TPU v7x, 256 devices: a whole 4x4x8 slice. The times are simulated.
256 devices in a mesh: tm: 8 (over z_lo, core), view: 8 (over z_hi, y), space: 4 (over x).
Axes of the slice: x: 4, y: 4, z: 8 (z_hi: 2, z_lo: 4; z = z_hi * 4 + z_lo), core: 2. Of those that a mesh axis runs over, the one named last changes fastest.
Arguments:
- latents: bfloat16 [8, 8, 512, 768], P('view', 'tm', 'space'), may hold values from -6 to 6
- cotangent: bfloat16 [8, 8, 512, 768], P('view', 'tm', 'space'), may hold values from -6 to 6
- w_qkv_space: bfloat16 [3, 768, 768], P(None, 'space'), may hold values from -1 to 1
- w_out_space: bfloat16 [768, 768], P('space'), may hold values from -0.21875 to 0.21875
- w_qkv_view: bfloat16 [3, 768, 768], P(None, 'space'), may hold values from -1 to 1
- w_out_view: bfloat16 [768, 768], P('space'), may hold values from -0.21875 to 0.21875
- w_qkv_time: bfloat16 [3, 768, 768], P(None, 'space'), may hold values from -1 to 1
- w_out_time: bfloat16 [768, 768], P('space'), may hold values from -0.21875 to 0.21875
Outputs:
- grad_latents: bfloat16 [8, 8, 512, 768], P('view', 'tm', 'space')
All inputs are finite; a program needn't handle non-finite values.
Results may differ from a plain program's by a relative error of at most 0.025.
Values may be sent and summed in bfloat16 or wider, within the bound.
A program may use at most 128 MiB of HBM per device.

v0:
```python
from functools import partial

import jax
import jax.numpy as jnp
from jax import lax
from jax.sharding import PartitionSpec as P

HEADS = 12


def rms_rows(stream):
    values = stream.astype(jnp.float32)
    factor = lax.rsqrt(jnp.mean(values * values, axis=-1, keepdims=True) + 1e-06)
    return (values * factor, factor)


def spatial_forward(packed):
    scale = packed.shape[-1] ** (-0.5)
    scores = (
        jnp.einsum("qhe,khe->hqk", packed[:, 0], packed[:, 1], preferred_element_type=jnp.float32)
        * scale
    )
    top = jnp.max(scores, axis=-1, keepdims=True)
    expo = jnp.exp(scores - top)
    shares = expo / jnp.sum(expo, axis=-1, keepdims=True)
    rounded = shares.astype(jnp.bfloat16)
    output = jnp.einsum(
        "hqk,khe->qhe", rounded, packed[:, 2], preferred_element_type=jnp.float32
    ).astype(jnp.bfloat16)
    return (output, (packed, output, rounded, shares))


def spatial_backward(saved, out_grad):
    packed, output, rounded, shares = saved
    scale = packed.shape[-1] ** (-0.5)
    row_dot = jnp.sum(out_grad.astype(jnp.float32) * output.astype(jnp.float32), axis=-1)
    share_grad = jnp.einsum(
        "qhe,khe->hqk", out_grad, packed[:, 2], preferred_element_type=jnp.float32
    )
    score_grad = shares * (share_grad - row_dot.T[:, :, None])
    rounded_grad = score_grad.astype(jnp.bfloat16)
    query_grad = (
        jnp.einsum("hqk,khe->qhe", rounded_grad, packed[:, 1], preferred_element_type=jnp.float32)
        * scale
    )
    key_grad = (
        jnp.einsum("hqk,qhe->khe", rounded_grad, packed[:, 0], preferred_element_type=jnp.float32)
        * scale
    )
    value_grad = jnp.einsum("hqk,qhe->khe", rounded, out_grad, preferred_element_type=jnp.float32)
    return jnp.stack([query_grad, key_grad, value_grad], axis=1).astype(jnp.bfloat16)


def small_forward(queries, key_rows, value_rows):
    scale = queries.shape[-1] ** (-0.5)
    scores = (
        jnp.einsum("athe,bthe->abth", queries, key_rows, preferred_element_type=jnp.float32) * scale
    )
    top = jnp.max(scores, axis=1, keepdims=True)
    expo = jnp.exp(scores - top)
    shares = expo / jnp.sum(expo, axis=1, keepdims=True)
    output = jnp.einsum("abth,bthe->athe", shares, value_rows.astype(jnp.float32)).astype(
        jnp.bfloat16
    )
    return (output, shares)


def small_backward(queries, key_rows, value_rows, output, out_grad, shares):
    scale = queries.shape[-1] ** (-0.5)
    grad_f = out_grad.astype(jnp.float32)
    row_dot = jnp.sum(grad_f * output.astype(jnp.float32), axis=-1)
    share_grad = jnp.einsum(
        "athe,bthe->abth", out_grad, value_rows, preferred_element_type=jnp.float32
    )
    score_grad = shares * (share_grad - row_dot[:, None])
    query_grad = jnp.einsum("abth,bthe->athe", score_grad, key_rows.astype(jnp.float32)) * scale
    key_grad = jnp.einsum("abth,athe->bthe", score_grad, queries.astype(jnp.float32)) * scale
    value_grad = jnp.einsum("abth,athe->bthe", shares, grad_f)
    return (query_grad, key_grad, value_grad)


def gather_forward(packed, keys_fn):
    gathered = keys_fn(packed[None, :, 1:])
    queries = packed[None, :, 0]
    output, shares = small_forward(queries, gathered[:, :, 0], gathered[:, :, 1])
    return (output[0], (queries, gathered, output, shares))


def gather_backward(saved, out_grad, grads_fn):
    queries, gathered, output, shares = saved
    query_grad, key_grad, value_grad = small_backward(
        queries, gathered[:, :, 0], gathered[:, :, 1], output, out_grad[None], shares
    )
    summed = grads_fn(jnp.stack([key_grad, value_grad], axis=2))
    return jnp.concatenate([query_grad[:, :, None], summed], axis=2)[0].astype(jnp.bfloat16)


def on_device(
    latents, cotangent, w_qkv_space, w_out_space, w_qkv_view, w_out_view, w_qkv_time, w_out_time
):
    width = latents.shape[-1]
    head_dim = width // HEADS

    def spread(rows, matrix):
        return lax.dot_general(
            lax.all_gather(rows, "space", axis=0, tiled=True),
            matrix,
            (((1,), (1,)), ((), ())),
            preferred_element_type=jnp.float32,
        ).astype(jnp.bfloat16)

    def collect(whole, matrix, count):

        def term(start, size):
            return jnp.dot(whole, matrix, preferred_element_type=jnp.float32)

        return lax.psum_scatter(
            term(jnp.int32(0), count * lax.axis_size("space")),
            "space",
            scatter_dimension=0,
            tiled=True,
        )

    def views_keys(moving):
        return lax.all_gather(moving, "view", axis=0, tiled=True)

    def views_grads(moving):
        return lax.psum_scatter(
            moving.astype(jnp.bfloat16), "view", scatter_dimension=0, tiled=True
        ).astype(jnp.float32)

    view_ops = (
        partial(gather_forward, keys_fn=views_keys),
        partial(gather_backward, grads_fn=views_grads),
    )

    def frames_keys(moving):
        return lax.all_gather(moving, "tm", axis=0, tiled=True)

    def frames_grads(moving):
        return lax.psum_scatter(
            moving.astype(jnp.bfloat16), "tm", scatter_dimension=0, tiled=True
        ).astype(jnp.float32)

    time_ops = (
        partial(gather_forward, keys_fn=frames_keys),
        partial(gather_backward, grads_fn=frames_grads),
    )
    layers = (
        (w_qkv_space, w_out_space, (spatial_forward, spatial_backward)),
        (w_qkv_view, w_out_view, view_ops),
        (w_qkv_time, w_out_time, time_ops),
    )
    stream = latents[0, 0]
    tok_rows = stream.shape[0]
    saved_all = []
    for position in range(3):
        w_qkv, w_out, layer_ops = layers[position]
        normed, factor = rms_rows(stream)
        packed = spread(normed.astype(jnp.bfloat16), w_qkv.reshape(-1, width))
        seq_rows = packed.shape[0]
        packed = packed.reshape(seq_rows, 3, -1, head_dim)
        output, context = layer_ops[0](packed)
        saved_all.append((stream, context))
        if position < 2:
            term = collect(output.reshape(seq_rows, -1), w_out, tok_rows)
            stream = (stream.astype(jnp.float32) + term).astype(jnp.bfloat16)
    upstream = cotangent[0, 0]
    for position in (2, 1, 0):
        w_qkv, w_out, layer_ops = layers[position]
        earlier, context = saved_all[position]
        out_grad = spread(upstream, w_out)
        out_grad = out_grad.reshape(out_grad.shape[0], -1, head_dim)
        packed_grad = layer_ops[1](context, out_grad)
        normed_grad = collect(
            packed_grad.reshape(packed_grad.shape[0], -1), w_qkv.reshape(-1, width), tok_rows
        )
        normed, factor = rms_rows(earlier)
        inner = jnp.mean(normed_grad * normed, axis=-1, keepdims=True)
        upstream = (upstream.astype(jnp.float32) + factor * (normed_grad - normed * inner)).astype(
            jnp.bfloat16
        )
    return upstream[None, None]


def solution(mesh):
    in_specs = (
        P("view", "tm", "space", None),
        P("view", "tm", "space", None),
        P(None, "space", None),
        P("space", None),
        P(None, "space", None),
        P("space", None),
        P(None, "space", None),
        P("space", None),
    )
    out_specs = P("view", "tm", "space", None)
    return jax.shard_map(
        on_device, mesh=mesh, in_specs=in_specs, out_specs=out_specs, check_vma=False
    )
```

profile of v0, /device:TPU:2, one launch (start us, length us, event | category | flops | bytes accessed | tf_op | source)
XLA Modules:
  0.0 631.3 jit_solution(10661192658028492264)
XLA Ops:
  9.2 14.2 %all_gather.24 = bf16[512,768]{1,0:T(8,128)(2,1)S(1)} all-gather(bf16[128,768]{1,0:T(8,128)(2,1)S(1)} %fusion.21), channel_id=1, replica_groups=mesh['tm'=8,'view'=8,'space'=4] {'space'}, dimensions={0}, use_global_device_ids=true | all-gather | bytes 983040 | tf_op jit(solution)/shard_map/all_gather | solution.py:106
  25.2 2.8 fusion.66
  28.7 2.4 fusion.9
  33.1 29.6 %reduce-scatter.10.cloned.1.call-done = f32[128,768]{1,0:T(8,128)} async-done(((f32[512,768]{1,0:T(8,128)}), f32[128,768]{1,0:T(8,128)}) %reduce-scatter.10.cloned.1.call-update) | async-done | bytes 393232 | tf_op jit(solution)/shard_map/reduce_scatter | solution.py:117
  64.0 14.1 %all_gather.25 = bf16[512,768]{1,0:T(8,128)(2,1)S(1)} all-gather(bf16[128,768]{1,0:T(8,128)(2,1)S(1)} %fusion.18), channel_id=1, replica_groups=mesh['tm'=8,'view'=8,'space'=4] {'space'}, dimensions={0}, use_global_device_ids=true | all-gather | bytes 983040 | tf_op jit(solution)/shard_map/all_gather | solution.py:106
  82.5 94.0 %all-gather.6.cloned.1.call-done = bf16[4096,2,3,64]{0,3,2,1:T(8,128)(2,1)} async-done(((bf16[512,2,3,64]{0,3,2,1:T(8,128)(2,1)}), bf16[4096,2,3,64]{0,3,2,1:T(8,128)(2,1)}) %all-gather.6.cloned.1.call-update) | async-done | bytes 3145744 | tf_op jit(solution)/shard_map/all_gather | solution.py:125
  176.6 3.3 copy.98
  185.2 22.7 %reduce-scatter.12.cloned.1.call-done = f32[128,768]{1,0:T(8,128)} async-done(((f32[512,768]{1,0:T(8,128)}), f32[128,768]{1,0:T(8,128)}) %reduce-scatter.12.cloned.1.call-update) | async-done | bytes 393232 | tf_op jit(solution)/shard_map/reduce_scatter | solution.py:117
  209.2 14.0 %all_gather.27 = bf16[512,768]{1,0:T(8,128)(2,1)S(1)} all-gather(bf16[128,768]{1,0:T(8,128)(2,1)S(1)} %fusion.24), channel_id=1, replica_groups=mesh['tm'=8,'view'=8,'space'=4] {'space'}, dimensions={0}, use_global_device_ids=true | all-gather | bytes 983040 | tf_op jit(solution)/shard_map/all_gather | solution.py:106
  225.6 13.7 %all-gather.2 = bf16[1,1,512,768]{3,2,1,0:T(8,128)(2,1)S(1)} all-gather(bf16[1,1,128,768]{3,2,1,0:T(8,128)(2,1)} %param.9), channel_id=4, replica_groups=mesh['tm'=8,'view'=8,'space'=4] {'space'}, dimensions={2}, use_global_device_ids=true | all-gather | bytes 983040 | tf_op jit(solution)/shard_map/all_gather | solution.py:106
  243.9 27.9 %all-gather.8.cloned.1.call-done = bf16[4096,2,3,64]{0,3,2,1:T(8,128)(2,1)} async-done(((bf16[512,2,3,64]{0,3,2,1:T(8,128)(2,1)}), bf16[4096,2,3,64]{0,3,2,1:T(8,128)(2,1)}) %all-gather.8.cloned.1.call-update) | async-done | bytes 3145744 | tf_op jit(solution)/shard_map/all_gather | solution.py:138
  271.7 3.4 copy.99
  279.9 2.4 multiply_reduce_fusion.2
  283.0 41.4 %reduce-scatter.14.cloned.1.call-done = bf16[1,512,2,3,64]{1,4,3,2,0:T(8,128)(2,1)} async-done(((bf16[8,512,2,3,64]{1,4,3,2,0:T(8,128)(2,1)}), bf16[1,512,2,3,64]{1,4,3,2,0:T(8,128)(2,1)}) %reduce-scatter.14.cloned.1.call-update) | async-done | bytes 393232 | tf_op jit(solution)/shard_map/reduce_scatter | solution.py:141
  325.6 2.0 fusion.69
  327.6 26.7 %reduce-scatter.16.cloned.1.call-done = f32[128,768]{1,0:T(8,128)} async-done(((f32[512,768]{1,0:T(8,128)}), f32[128,768]{1,0:T(8,128)}) %reduce-scatter.16.cloned.1.call-update) | async-done | bytes 393232 | tf_op jit(solution)/shard_map/reduce_scatter | solution.py:117
  357.6 14.1 %all_gather.30 = bf16[512,768]{1,0:T(8,128)(2,1)S(1)} all-gather(bf16[128,768]{1,0:T(8,128)(2,1)S(1)} %fusion.29), channel_id=1, replica_groups=mesh['tm'=8,'view'=8,'space'=4] {'space'}, dimensions={0}, use_global_device_ids=true | all-gather | bytes 983040 | tf_op jit(solution)/shard_map/all_gather | solution.py:106
  377.7 2.4 multiply_reduce_fusion
  380.2 157.4 %all-reduce.3.cloned.1.call-done = bf16[8,512,2,3,64]{1,4,3,0,2:T(8,128)(2,1)} async-done(((bf16[8,512,2,3,64]{1,4,3,0,2:T(8,128)(2,1)}), bf16[8,512,2,3,64]{1,4,3,0,2:T(8,128)(2,1)}) %all-reduce.3.cloned.1.call-update) | async-done | bytes 3145744
  539.3 3.1 fusion.70
  542.5 28.4 %reduce-scatter.18.cloned.1.call-done = f32[128,768]{1,0:T(8,128)} async-done(((f32[512,768]{1,0:T(8,128)}), f32[128,768]{1,0:T(8,128)}) %reduce-scatter.18.cloned.1.call-update) | async-done | bytes 393232 | tf_op jit(solution)/shard_map/reduce_scatter | solution.py:117
  573.5 14.2 %all_gather.31 = bf16[512,768]{1,0:T(8,128)(2,1)S(1)} all-gather(bf16[128,768]{1,0:T(8,128)(2,1)S(1)} %fusion.40), channel_id=1, replica_groups=mesh['tm'=8,'view'=8,'space'=4] {'space'}, dimensions={0}, use_global_device_ids=true | all-gather | bytes 983040 | tf_op jit(solution)/shard_map/all_gather | solution.py:106
  591.5 2.0 fusion.71
  593.5 28.2 %reduce-scatter.20.cloned.1.call-done = f32[128,768]{1,0:T(8,128)} async-done(((f32[512,768]{1,0:T(8,128)}), f32[128,768]{1,0:T(8,128)}) %reduce-scatter.20.cloned.1.call-update) | async-done | bytes 393232 | tf_op jit(solution)/shard_map/reduce_scatter | solution.py:117
  (165 shorter events, 53.1 us)
Async XLA Ops:
  6.5 216.7 %copy-start = (bf16[3,192,768]{2,1,0:T(8,128)(2,1)S(1)}, bf16[3,192,768]{2,1,0:T(8,128)(2,1)}, u32[]{:S(2)}) copy-start(bf16[3,192,768]{2,1,0:T(8,128)(2,1)} %param.14) | copy-start | bytes 2654212
  6.5 56.2 %reduce-scatter.10.cloned.1.call-start = ((), (), s32[]{:S(2)}) async-start(), calls=%async_computation.6 | async-start | bytes 1966080 | tf_op jit(solution)/shard_map/reduce_scatter | solution.py:117
  31.1 31.6 %copy-start.4 = (bf16[1,1,128,768]{3,2,1,0:T(8,128)(2,1)S(1)}, bf16[1,1,128,768]{3,2,1,0:T(8,128)(2,1)}, u32[]{:S(2)}) copy-start(bf16[1,1,128,768]{3,2,1,0:T(8,128)(2,1)} %param.8) | copy-start | bytes 589828
  33.1 143.5 %all-gather.6.cloned.1.call-start = ((), (), s32[]{:S(2)}) async-start(), calls=%async_computation.12 | async-start | bytes 3538944 | tf_op jit(solution)/shard_map/all_gather | solution.py:125
  63.9 14.2 %copy-start.33 = (f32[128]{0:T(128)}, f32[128]{0:T(128)S(1)}, u32[]{:S(2)}) copy-start(f32[128]{0:T(128)S(1)} %add_rsqrt_fusion.1) | copy-start | bytes 1540
  81.5 126.4 %reduce-scatter.12.cloned.1.call-start = ((), (), s32[]{:S(2)}) async-start(), calls=%async_computation.7 | async-start | bytes 1966080 | tf_op jit(solution)/shard_map/reduce_scatter | solution.py:117
  185.2 86.6 %all-gather.8.cloned.1.call-start = ((), (), s32[]{:S(2)}) async-start(), calls=%async_computation.13 | async-start | bytes 3538944 | tf_op jit(solution)/shard_map/all_gather | solution.py:138
  209.1 14.2 %copy-start.35 = (f32[128]{0:T(128)}, f32[128]{0:T(128)S(1)}, u32[]{:S(2)}) copy-start(f32[128]{0:T(128)S(1)} %add_rsqrt_fusion) | copy-start | bytes 1540
  225.5 98.9 %reduce-scatter.14.cloned.1.call-start = ((), (), s32[]{:S(2)}) async-start(), calls=%async_computation.8 | async-start | bytes 3538944 | tf_op jit(solution)/shard_map/reduce_scatter | solution.py:141
  279.9 74.4 %reduce-scatter.16.cloned.1.call-start = ((), (), s32[]{:S(2)}) async-start(), calls=%async_computation.9 | async-start | bytes 1966080 | tf_op jit(solution)/shard_map/reduce_scatter | solution.py:117
  282.3 72.0 %copy-start.36 = (f32[128]{0:T(128)S(1)}, f32[128]{0:T(128)}, u32[]{:S(2)}) copy-start(f32[128]{0:T(128)} %copy-done.35) | copy-start | bytes 1540
  327.6 210.0 %all-reduce.3.cloned.1.call-start = ((), (), s32[]{:S(2)}) async-start(), calls=%async_computation.14 | async-start | bytes 6291456
  354.3 18.8 %copy-start.13 = (bf16[512,3,64]{0,2,1:T(8,128)(2,1)S(1)}, bf16[512,3,64]{0,2,1:T(8,128)(2,1)}, u32[]{:S(2)}) copy-start(bf16[512,3,64]{0,2,1:T(8,128)(2,1)} %copy-done.12) | copy-start | bytes 589828
  354.3 19.0 %copy-start.2 = (bf16[48,8,8,512]{3,2,1,0:T(8,128)(2,1)S(1)}, bf16[48,8,8,512]{3,2,1,0:T(8,128)(2,1)}, u32[]{:S(2)}) copy-start(bf16[48,8,8,512]{3,2,1,0:T(8,128)(2,1)} %copy-done.1) | copy-start | bytes 9437188
  355.6 17.9 %copy-start.20 = (f32[512,3,8]{0,1,2:T(4,128)S(1)}, f32[512,3,8]{0,1,2:T(4,128)}, u32[]{:S(2)}) copy-start(f32[512,3,8]{0,1,2:T(4,128)} %copy-done.19) | copy-start | bytes 147460
  376.4 194.5 %reduce-scatter.18.cloned.1.call-start = ((), (), s32[]{:S(2)}) async-start(), calls=%async_computation.10 | async-start | bytes 1966080 | tf_op jit(solution)/shard_map/reduce_scatter | solution.py:117
  537.5 33.4 %copy-start.34 = (f32[128]{0:T(128)S(1)}, f32[128]{0:T(128)}, u32[]{:S(2)}) copy-start(f32[128]{0:T(128)} %copy-done.33) | copy-start | bytes 1540
  539.2 33.0 %copy-start.11 = (bf16[128,768]{1,0:T(8,128)(2,1)S(1)}, bf16[128,768]{1,0:T(8,128)(2,1)}, u32[]{:S(2)}) copy-start(bf16[128,768]{1,0:T(8,128)(2,1)} %copy-done.10) | copy-start | bytes 589828
  542.5 46.6 %copy-start.15 = (bf16[3,64,512]{2,1,0:T(8,128)(2,1)S(1)}, bf16[3,64,512]{2,1,0:T(8,128)(2,1)}, u32[]{:S(2)}) copy-start(bf16[3,64,512]{2,1,0:T(8,128)(2,1)} %copy-done.14) | copy-start | bytes 589828
  542.5 46.7 %copy-start.30 = (f32[3,512]{1,0:T(4,128)S(1)}, f32[3,512]{1,0:T(4,128)}, u32[]{:S(2)}) copy-start(f32[3,512]{1,0:T(4,128)} %copy-done.29) | copy-start | bytes 18436
  542.5 79.2 %reduce-scatter.20.cloned.1.call-start = ((), (), s32[]{:S(2)}) async-start(), calls=%async_computation.11 | async-start | bytes 1966080 | tf_op jit(solution)/shard_map/reduce_scatter | solution.py:117
  570.9 18.3 %copy-start.7 = (f32[3,512,512]{1,2,0:T(8,128)S(1)}, f32[3,512,512]{1,2,0:T(8,128)}, u32[]{:S(2)}) copy-start(f32[3,512,512]{1,2,0:T(8,128)} %get-tuple-element.12) | copy-start | bytes 9437188
  570.9 18.3 %copy-start.24 = (bf16[512,576]{0,1:T(8,128)(2,1)S(1)}, bf16[512,576]{0,1:T(8,128)(2,1)}, u32[]{:S(2)}) copy-start(bf16[512,576]{0,1:T(8,128)(2,1)} %copy-done.23) | copy-start | bytes 1769476
  591.4 30.3 %copy-start.32 = (f32[128]{0:T(128)S(1)}, f32[128]{0:T(128)}, u32[]{:S(2)}) copy-start(f32[128]{0:T(128)} %copy-done.31) | copy-start | bytes 1540
  (23 other events, 43.1 us)
Sparse Core Ops, SparseCore 0:
  33.2 29.4 reduce-scatter.9
  81.6 94.9 all-gather.5
  185.3 22.6 reduce-scatter.11
  225.7 46.0 all-gather.7
  280.0 44.4 reduce-scatter.13
  327.7 26.5 reduce-scatter.15
  376.5 160.9 all-reduce.2
  542.6 28.2 reduce-scatter.17
  593.6 28.0 reduce-scatter.19
where the time goes:
time: 633 us; the launch traced here: 631 us
  waiting for transfers between devices  456 us (72%)
  blocking collectives  84.3 us (13%)
  other arithmetic  34.7 us (5%)
  matrix products  24 us (4%)
  local copies, waits for them, and re-layouts  17.6 us (3%)
  between operations  13.9 us (2%)
    unnamed x10, waiting for transfers between devices  158 us
    reduce_scatter x5, waiting for transfers between devices, collect(): lax.psum_scatter(term(jnp.int32(0), count * lax.axis_size('space')), 'spa...  136 us
    all_gather x1, waiting for transfers between devices, views_keys(): return lax.all_gather(moving, 'view', axis=0, tiled=True)  94 us
    all_gather x6, blocking collectives, spread(): lax.all_gather(rows, 'space', axis=0, tiled=True)  84.3 us
    reduce_scatter x1, waiting for transfers between devices, frames_grads(): lax.psum_scatter(moving.astype(jnp.bfloat16), 'tm', scatter_dimension=0,...  41.4 us
    all_gather x1, waiting for transfers between devices, frames_keys(): return lax.all_gather(moving, 'tm', axis=0, tiled=True)  27.9 us
    unnamed x83, local copies, waits for them, and re-layouts  14.3 us
  transfers between devices with their start and end apart: 9, of which 9 were waited for; matrix products, arithmetic and copies ran while one was open for 2% of the time, Pallas kernels for 0%

commit v1 on v0

v1 whole, which is shorter than its diff:
```python
import jax
import jax.numpy as jnp
from jax import lax
from jax.experimental import pallas as pl
from jax.experimental.pallas import tpu as pltpu
from jax.sharding import PartitionSpec as P

MESH = pl.DeviceIdType.MESH
BF = jnp.bfloat16
F32 = jnp.float32
NN = ((1,), (0,))
NT = ((1,), (1,))
TN = ((0,), (0,))

D = 768
TOK = 128
NSP = 4
NV = 8
NT_ = 8
CH = 16
HD = 64
LH = 3
LW = LH * HD
GH = 4
GW = GH * HD
GROUPS = D // GW
SCALE = HD**-0.5
NSEM = 208


def dot(a, b, dims):
    return lax.dot_general(a, b, (dims, ((), ())), preferred_element_type=F32)


def rms(values):
    factor = lax.rsqrt(jnp.mean(values * values, axis=-1, keepdims=True) + 1e-06)
    return values * factor, factor


def finish(upstream, earlier, normed_grad):
    normed, factor = rms(earlier.astype(F32))
    inner = jnp.mean(normed_grad * normed, axis=-1, keepdims=True)
    return (upstream.astype(F32) + factor * (normed_grad - normed * inner)).astype(BF)


def softmax0(scores):
    top = jnp.max(scores, axis=0, keepdims=True)
    expo = jnp.exp(scores - top)
    return expo * (1.0 / jnp.sum(expo, axis=0, keepdims=True))


def head_masks(rows):
    head = lax.broadcasted_iota(jnp.int32, (rows, TOK), 0) // HD
    return [(head == h).astype(F32).astype(BF) for h in range(rows // HD)]


def stacked(values, masks):
    return jnp.concatenate([values * m for m in masks], axis=1)


def per_head(left, right):
    heads = left.shape[0] // HD
    return jnp.concatenate(
        [
            dot(left[h * HD : (h + 1) * HD], right[:, h * TOK : (h + 1) * TOK], NN)
            for h in range(heads)
        ],
        axis=0,
    )


def body(
    x_in, cot_in, wqs_in, wos_in, wqv_in, wov_in, wqt_in, wot_in,
    out_ref,
    x_ref, cot_ref, wqs_ref,
    nb, k_nat, v_nat, qts, kvt, pts, gts, ogts, dqt, ats, att,
    xb, x2, xt, x3, c1, c2, ut, u2, uv, u3, ogs, og, rsend, rs, rf,
    bias, kt_v, vt_v, qts_v, pt_v,
    wos, wqv, wov, wqt, wot,
    send_sem, recv_sem, local_sem,
):
    t = lax.axis_index("tm")
    v = lax.axis_index("view")
    s = lax.axis_index("space")
    core = lax.rem(t, 2)
    sibling = t + 1 - 2 * core
    y = lax.rem(v, 4)
    half = lax.rem(y, 2)
    step = 1 - 2 * core
    y_next = v - y + lax.rem(y + step + 4, 4)
    s_next = lax.rem(s + step + 4, 4)
    s_prev = lax.rem(s - step + 4, 4)

    def plus(me, k, n):
        return lax.rem(me + k + n, n)

    sent = []
    count = [0]

    def ticket():
        count[0] += 1
        return count[0] - 1

    def push(src, dst, axis, index, number):
        to = {axis: index} if isinstance(axis, str) else dict(zip(axis, index))
        copy = pltpu.make_async_remote_copy(
            src_ref=src,
            dst_ref=dst,
            send_sem=send_sem.at[number],
            recv_sem=recv_sem.at[number],
            device_id=to,
            device_id_type=MESH,
        )
        copy.start()
        sent.append(copy)

    def landed(dst, number, axis, index):
        to = {axis: index} if isinstance(axis, str) else dict(zip(axis, index))
        pltpu.make_async_remote_copy(
            src_ref=dst,
            dst_ref=dst,
            send_sem=send_sem.at[number],
            recv_sem=recv_sem.at[number],
            device_id=to,
            device_id_type=MESH,
        ).wait_recv()

    def rows(owner, c, h, size):
        return pl.ds(pl.multiple_of(owner * LW + c * 96 + h * 48, 16), size)

    class Gather:
        def __init__(self, shard, full, number):
            self.shard, self.full = shard, full
            self.x1 = [ticket(), ticket()]
            self.x2 = ticket()
            self.ys = [ticket() for _ in range(3)]
            self.sib = [ticket() for _ in range(3)]
            self.others = [plus(s, -1, 4), plus(s, 1, 4), plus(s, 2, 4)]
            self.own = pltpu.make_async_copy(
                shard, full.at[:, pl.ds(pl.multiple_of(s * LW, 16), LW), :], local_sem.at[number]
            )

        def piece(self, owner, c, h, size=48):
            return self.full.at[:, rows(owner, c, h, size), :]

        def a(self):
            self.own.start()
            mine = self.shard.at[:, pl.ds(pl.multiple_of(core * 96 + half * 48, 16), 48), :]
            there = self.piece(s, core, half)
            push(mine, there, "space", plus(s, 1, 4), self.x1[0])
            push(mine, there, "space", plus(s, -1, 4), self.x1[1])

        def b(self):
            for at in range(2):
                landed(self.piece(self.others[at], core, half), self.x1[at], "space", self.others[at])
            far = self.piece(s_prev, core, half)
            push(far, far, "space", s_next, self.x2)
            for at in range(2):
                part = self.piece(self.others[at], core, half)
                push(part, part, "view", y_next, self.ys[at])

        def c(self):
            part = self.piece(self.others[2], core, half)
            landed(part, self.x2, "space", s_prev)
            push(part, part, "view", y_next, self.ys[2])

        def d(self):
            for at in range(3):
                landed(self.piece(self.others[at], core, 1 - half), self.ys[at], "view", y_next)
                part = self.piece(self.others[at], core, 0, 96)
                push(part, part, "tm", sibling, self.sib[at])

        def e(self):
            for at in range(3):
                landed(self.piece(self.others[at], 1 - core, 0, 96), self.sib[at], "tm", sibling)
            self.own.wait()

    g_os = Gather(wos_in, wos, 0)
    g_qv = Gather(wqv_in, wqv, 1)
    g_ov = Gather(wov_in, wov, 2)
    g_qt = Gather(wqt_in, wqt, 3)
    g_ot = Gather(wot_in, wot, 4)

    loads = [
        pltpu.make_async_copy(src, dst, local_sem.at[5 + at])
        for at, (src, dst) in enumerate(((x_in, x_ref), (wqs_in, wqs_ref), (cot_in, cot_ref)))
    ]
    for copy in loads:
        copy.start()

    barrier = pltpu.get_barrier_semaphore()
    for k in range(NSP):
        for j in range(NV):
            if k or j:
                pl.semaphore_signal(
                    barrier,
                    inc=1,
                    device_id={"view": plus(v, j, NV), "space": plus(s, k, NSP)},
                    device_id_type=MESH,
                )
    for k in range(1, NT_):
        pl.semaphore_signal(barrier, inc=1, device_id={"tm": plus(t, k, NT_)}, device_id_type=MESH)

    loads[0].wait()
    x_rows = x_ref[...].reshape(TOK, D)
    normed, _ = rms(x_rows.astype(F32))
    nb[0] = normed.astype(BF)
    key_at = lax.broadcasted_iota(jnp.int32, (TOK, GH * TOK), 0)
    query_at = lax.broadcasted_iota(jnp.int32, (TOK, GH * TOK), 1)
    bias[...] = jnp.where(lax.rem(key_at, CH) == lax.rem(query_at, CH), 0.0, -1e30)
    lmask = head_masks(LW)
    gmask = head_masks(GW)
    pl.semaphore_wait(barrier, NSP * NV + NT_ - 2)

    halves = [slice(0, TOK // 2), slice(TOK // 2, TOK)]
    n_num = [{k: ticket() for k in range(1, NSP)} for _ in halves]
    for h, part in enumerate(halves):
        for k in (1, 3):
            push(nb.at[0, part], nb.at[k, part], "space", plus(s, k, NSP), n_num[h][k])
    loads[1].wait()
    loads[2].wait()
    g_os.a()
    order = (4, 3, 5, 2, 6, 1, 7)
    x2_num = [ticket() for _ in range(NV)]
    c1_num = [ticket() for _ in range(NV)]
    for j in order:
        to = plus(v, j, NV)
        push(x_ref.at[to], xb.at[j], "view", to, x2_num[j])
    for j in order:
        to = plus(v, j, NV)
        push(cot_ref.at[to], c1.at[j], "view", to, c1_num[j])
    xb[0] = x_ref[v]
    c1[0] = cot_ref[v]

    def project_space(k):
        tokens = nb[k]
        packed = dot(wqs_ref[...], tokens, NT)
        at = slice(k * TOK, (k + 1) * TOK)
        query = packed[:LW].astype(BF) * jnp.asarray(SCALE, BF)
        qts[:, k * LH * TOK : (k + 1) * LH * TOK] = stacked(query, lmask)
        kvt[:, at] = packed[LW:].astype(BF)
        k_nat[at, :] = jnp.transpose(packed[LW : 2 * LW]).astype(BF)
        v_nat[at, :] = jnp.transpose(packed[2 * LW :]).astype(BF)

    project_space(0)
    for h, part in enumerate(halves):
        for k in (1, 3):
            landed(nb.at[k, part], n_num[h][k], "space", plus(s, -k, NSP))
        push(nb.at[1 + 2 * core, part], nb.at[2, part], "space", s_next, n_num[h][2])
    g_qv.a()
    project_space(1)
    project_space(3)
    g_os.b()
    for h, part in enumerate(halves):
        landed(nb.at[2, part], n_num[h][2], "space", plus(s, 2, NSP))
    project_space(2)

    a_num = [[ticket() for _ in range(NV)] for _ in range(NSP)]

    def attend_space(k):
        at = slice(k * LH * TOK, (k + 1) * LH * TOK)
        shares = softmax0(dot(k_nat[...], qts[:, at], NN)).astype(BF)
        pts[:, at] = shares
        out = jnp.transpose(per_head(kvt[LW:, :], shares)).astype(BF)
        ats[k] = out.reshape(NV, CH, LW)
        for j in order + (0,):
            to = (plus(v, j, NV), plus(s, -k, NSP))
            if k or j:
                push(ats.at[k, to[0]], att.at[s, j], ("view", "space"), to, a_num[k][j])
            else:
                att[pl.ds(s, 1), 0:1] = ats[0:1, pl.ds(v, 1)]

    attend_space(2)
    g_qv.b()
    g_os.c()
    g_ov.a()
    g_ot.a()
    attend_space(1)
    attend_space(3)
    g_qv.c()
    g_ov.b()
    g_ot.b()
    attend_space(0)
    g_os.d()
    g_qt.a()
    g_ov.c()
    g_ot.c()

    def slot_of(view):
        return lax.rem(v - view + NV, NV)

    c2_num = [ticket() for _ in range(NT_)]
    for k in range(1, NV):
        landed(c1.at[k], c1_num[k], "view", plus(v, -k, NV))
    for j in range(1, NT_):
        to = plus(t, j, NT_)
        push(c1.at[slot_of(to)], c2.at[j], "tm", to, c2_num[j])
    c2[0] = c1[slot_of(t)]
    g_qv.d()
    g_ov.d()
    g_ot.d()
    g_os.e()

    for j in range(1, NV):
        landed(xb.at[j], x2_num[j], "view", plus(v, -j, NV))
    for k in (2, 1, 3, 0):
        for j in range(NV):
            if k or j:
                group = plus(s, k, NSP)
                landed(att.at[group, j], a_num[k][j], ("view", "space"), (plus(v, -j, NV), group))
    term = dot(att[0].reshape(TOK, LW), wos[0, :LW, :], NN)
    for h in range(1, NSP):
        term += dot(att[h].reshape(TOK, LW), wos[0, h * LW : (h + 1) * LW, :], NN)
    x2[...] = (xb[...].reshape(TOK, D).astype(F32) + term).astype(BF).reshape(NV, CH, D)
    g_qt.b()
    rows_view = x2[...].reshape(TOK, D)
    normed, _ = rms(rows_view.astype(F32))
    tokens = normed.astype(BF)
    g_qv.e()

    def attend_small(w, g):
        lanes = slice(g * GW, (g + 1) * GW)
        query = dot(w[0, lanes, :], tokens, NT).astype(BF) * jnp.asarray(SCALE, BF)
        key_t = dot(w[1, lanes, :], tokens, NT).astype(BF)
        value_t = dot(w[2, lanes, :], tokens, NT).astype(BF)
        queries = stacked(query, gmask)
        shares = softmax0(dot(key_t, queries, TN) + bias[...]).astype(BF)
        return queries, key_t, value_t, shares

    def backward_small(w, g, queries, key_t, value_t, shares, out_grad):
        lanes = slice(g * GW, (g + 1) * GW)
        grads = stacked(out_grad, gmask)
        share_grad = dot(value_t, grads, TN)
        wide = shares.astype(F32)
        row_dot = jnp.sum(wide * share_grad, axis=0, keepdims=True)
        score_grad = (wide * (share_grad - row_dot)).astype(BF)
        query_grad = (per_head(key_t, score_grad) * SCALE).astype(BF)
        key_grad = dot(score_grad, queries, NT).astype(BF)
        value_grad = dot(shares, grads, NT).astype(BF)
        total = dot(query_grad, w[0, lanes, :], TN)
        total += dot(key_grad, w[1, lanes, :], NN)
        return total + dot(value_grad, w[2, lanes, :], NN)

    outs = []
    for g in range(GROUPS):
        queries, key_t, value_t, shares = attend_small(wqv, g)
        qts_v[g], kt_v[g], vt_v[g], pt_v[g] = queries, key_t, value_t, shares
        outs.append(per_head(value_t, shares).astype(BF))
        if g == 1:
            g_qt.c()
    g_ov.e()
    term = dot(jnp.concatenate(outs, axis=0), wov[0], TN)
    xt[...] = (rows_view.astype(F32) + term).astype(BF).reshape(NV, CH, D)

    x3_num = [ticket() for _ in range(NT_)]
    for j in range(1, NT_):
        to = plus(t, j, NT_)
        push(xt.at[slot_of(to)], x3.at[j], "tm", to, x3_num[j])
    x3[0] = xt[slot_of(t)]
    g_qt.d()
    for j in range(1, NT_):
        landed(c2.at[j], c2_num[j], "tm", plus(t, -j, NT_))
    for j in range(1, NT_):
        landed(x3.at[j], x3_num[j], "tm", plus(t, -j, NT_))
    rows_time = x3[...].reshape(TOK, D)
    normed, _ = rms(rows_time.astype(F32))
    tokens = normed.astype(BF)
    upstream = c2[...].reshape(TOK, D)
    g_qt.e()
    g_ot.e()

    total = jnp.zeros((TOK, D), F32)
    for g in range(GROUPS):
        queries, key_t, value_t, shares = attend_small(wqt, g)
        out_grad = dot(wot[0, g * GW : (g + 1) * GW, :], upstream, NT).astype(BF)
        total += backward_small(wqt, g, queries, key_t, value_t, shares, out_grad)
    ut[...] = finish(upstream, rows_time, total).reshape(NT_, CH, D)

    u2_num = [ticket() for _ in range(NT_)]
    here = slot_of(t)
    for j in range(1, NT_):
        push(ut.at[j], u2.at[here], "tm", plus(t, -j, NT_), u2_num[j])
    u2[pl.ds(here, 1)] = ut[0:1]
    for j in range(1, NT_):
        landed(u2.at[slot_of(plus(t, j, NT_))], u2_num[j], "tm", plus(t, j, NT_))
    upstream = u2[...].reshape(TOK, D)
    total = jnp.zeros((TOK, D), F32)
    for g in range(GROUPS):
        out_grad = dot(wov[0, g * GW : (g + 1) * GW, :], upstream, NT).astype(BF)
        total += backward_small(wqv, g, qts_v[g], kt_v[g], vt_v[g], pt_v[g], out_grad)
    upstream = finish(upstream, x2[...].reshape(TOK, D), total)
    uv[...] = upstream.reshape(NV, CH, D)

    out_grad = dot(wos[0], upstream, NT)
    for h in range(NSP):
        part = jnp.transpose(out_grad[h * LW : (h + 1) * LW]).astype(BF)
        ogs[h] = part.reshape(NV, CH, LW)
    og_num = [[ticket() for _ in range(NV)] for _ in range(NSP)]
    for k in (2, 1, 3, 0):
        for j in order + (0,):
            to = (plus(v, -j, NV), plus(s, k, NSP))
            if k or j:
                push(ogs.at[to[1], j], og.at[k, v], ("view", "space"), to, og_num[k][j])
    og[0:1, pl.ds(v, 1)] = ogs[pl.ds(s, 1), 0:1]
    u3_num = [ticket() for _ in range(NV)]
    for j in order:
        push(uv.at[j], u3.at[v], "view", plus(v, -j, NV), u3_num[j])
    u3[pl.ds(v, 1)] = uv[0:1]

    def backward_space(k):
        at = slice(k * LH * TOK, (k + 1) * LH * TOK)
        out_grad = og[k].reshape(TOK, LW)
        grads = jnp.concatenate([out_grad * m for m in nmask], axis=0)
        ogts[at, :] = grads
        share_grad = dot(v_nat[...], grads, NT)
        wide = pts[:, at].astype(F32)
        row_dot = jnp.sum(wide * share_grad, axis=0, keepdims=True)
        score_grad = (wide * (share_grad - row_dot)).astype(BF)
        gts[:, at] = score_grad
        dqt[k] = (per_head(kvt[:LW, :], score_grad) * SCALE).astype(BF)

    head_at = lax.broadcasted_iota(jnp.int32, (TOK, LW), 1) // HD
    nmask = [(head_at == h).astype(F32).astype(BF) for h in range(LH)]
    for k in (0, 1, 3, 2):
        for j in range(NV):
            if k or j:
                frm = (plus(v, j, NV), plus(s, -k, NSP))
                landed(og.at[k, frm[0]], og_num[k][j], ("view", "space"), frm)
        backward_space(k)

    def partial_sums(k):
        at = pl.ds(pl.multiple_of(k * TOK, TOK), TOK)
        key_grad = dot(gts[at, :], qts[...], NT).astype(BF)
        value_grad = dot(pts[at, :], ogts[...], NN).astype(BF)
        part = dot(dqt[k], wqs_ref[:LW, :], TN)
        part += dot(key_grad, wqs_ref[LW : 2 * LW, :], NN)
        return part + dot(value_grad, wqs_ref[2 * LW :, :], NN)

    rf_num, near_num, late_num = ticket(), ticket(), ticket()
    rsend[0] = partial_sums(2).astype(BF)
    push(rsend.at[0], rf, "space", s_next, rf_num)
    rsend[1] = partial_sums(1 + 2 * core).astype(BF)
    push(rsend.at[1], rs.at[0], "space", s_prev, near_num)
    late = partial_sums(3 - 2 * core)
    landed(rf, rf_num, "space", s_prev)
    rsend[2] = (late + rf[...].astype(F32)).astype(BF)
    push(rsend.at[2], rs.at[1], "space", s_next, late_num)
    total = partial_sums(0)
    landed(rs.at[0], near_num, "space", s_next)
    total += rs[0].astype(F32)
    landed(rs.at[1], late_num, "space", s_prev)
    total += rs[1].astype(F32)
    for j in range(1, NV):
        landed(u3.at[plus(v, j, NV)], u3_num[j], "view", plus(v, j, NV))
    out_ref[...] = finish(u3[...].reshape(TOK, D), x_ref[...].reshape(TOK, D), total)

    for copy in sent:
        copy.wait_send()


def on_device(latents, cotangent, wqs, wos, wqv, wov, wqt, wot):
    vmem = pl.BlockSpec(memory_space=pltpu.VMEM)
    hbm = pl.BlockSpec(memory_space=pltpu.HBM)

    def buf(*shape, dtype=BF):
        return pltpu.VMEM(shape, dtype)

    wide = NSP * LH * TOK
    out = pl.pallas_call(
        body,
        out_shape=jax.ShapeDtypeStruct((TOK, D), BF),
        in_specs=[hbm] * 8,
        out_specs=vmem,
        scratch_shapes=[
            buf(NV, CH, D),
            buf(NV, CH, D),
            buf(3 * LW, D),
            buf(NSP, TOK, D),
            buf(NSP * TOK, LW),
            buf(NSP * TOK, LW),
            buf(LW, wide),
            buf(2 * LW, NSP * TOK),
            buf(NSP * TOK, wide),
            buf(NSP * TOK, wide),
            buf(wide, LW),
            buf(NSP, LW, TOK),
            buf(NSP, NV, CH, LW),
            buf(NSP, NV, CH, LW),
        ]
        + [buf(NV, CH, D)] * 10
        + [
            buf(NSP, NV, CH, LW),
            buf(NSP, NV, CH, LW),
            buf(3, TOK, D),
            buf(2, TOK, D),
            buf(TOK, D),
            buf(TOK, GH * TOK, dtype=F32),
            buf(GROUPS, GW, TOK),
            buf(GROUPS, GW, TOK),
            buf(GROUPS, GW, GH * TOK),
            buf(GROUPS, TOK, GH * TOK),
            buf(1, D, D),
            buf(3, D, D),
            buf(1, D, D),
            buf(3, D, D),
            buf(1, D, D),
            pltpu.SemaphoreType.DMA((NSEM,)),
            pltpu.SemaphoreType.DMA((NSEM,)),
            pltpu.SemaphoreType.DMA((8,)),
        ],
        compiler_params=pltpu.CompilerParams(
            collective_id=0, has_side_effects=True, vmem_limit_bytes=60 * 1024 * 1024
        ),
        name="block_backward",
    )(
        latents.reshape(NV, CH, D),
        cotangent.reshape(NV, CH, D),
        wqs.reshape(3 * LW, D),
        wos[None],
        wqv,
        wov[None],
        wqt,
        wot[None],
    )
    return out[None, None]


def solution(mesh):
    in_specs = (
        P("view", "tm", "space", None),
        P("view", "tm", "space", None),
        P(None, "space", None),
        P("space", None),
        P(None, "space", None),
        P("space", None),
        P(None, "space", None),
        P("space", None),
    )
    return jax.shard_map(
        on_device,
        mesh=mesh,
        in_specs=in_specs,
        out_specs=P("view", "tm", "space", None),
        check_vma=False,
    )
```

time: 633 us -> 101 us (0.16)
  waiting for transfers between devices: 456 us -> 0 us
  Pallas kernels: 0 us -> 98.5 us
  blocking collectives: 84.3 us -> 0 us
  other arithmetic: 34.7 us -> 0 us
  matrix products: 24 us -> 0 us
  local copies, waits for them, and re-layouts: 17.6 us -> 1.62 us
  between operations: 13.9 us -> 0.01 us
    reduce_scatter x6 -> x0, waiting for transfers between devices: 177 us -> none  [the longest x5 136 us: collect(): lax.psum_scatter(term(jnp.int32(0), count * lax.axis_size('space')), 'spa...]
    unnamed x10 -> x0, waiting for transfers between devices: 158 us -> none
    all_gather x2 -> x0, waiting for transfers between devices: 122 us -> none  [the longest x1 94 us: views_keys(): return lax.all_gather(moving, 'view', axis=0, tiled=True)]
    pallas_call x0 -> x1, Pallas kernels: none -> 98.5 us  [on_device(): pl.pallas_call(body, out_shape=jax.ShapeDtypeStruct((TOK, D), BF), in_spe...]
    all_gather x6 -> x0, blocking collectives: 84.3 us -> none  [spread(): lax.all_gather(rows, 'space', axis=0, tiled=True)]
    dot_general x16 -> x0, matrix products: 21.2 us -> none  [the longest x5 10.2 us: term(): return jnp.dot(whole, matrix, preferred_element_type=jnp.float32)]
    unnamed x83 -> x1, local copies, waits for them, and re-layouts: 14.3 us -> 1.62 us
    reduce_sum x11 -> x0, other arithmetic: 7.61 us -> none  [the longest x3 3.87 us: on_device(): inner = jnp.mean(normed_grad * normed, axis=-1, keepdims=True)]
  transfers between devices with their start and end apart: 9 -> 0, of which waited for: 9 -> 0; matrix products, arithmetic and copies ran while one was open for 2% -> 0% of each run, Pallas kernels for 0% -> 0%
where the time goes in v1:
time: 101 us; the launch traced here: 100 us
  Pallas kernels  98.5 us (98%)
  local copies, waits for them, and re-layouts  1.62 us (2%)
    pallas_call x1, Pallas kernels, on_device(): pl.pallas_call(body, out_shape=jax.ShapeDtypeStruct((TOK, D), BF), in_spe...  98.5 us

profile of v1, /device:TPU:2, one launch (start us, length us, event | category | flops | bytes accessed | tf_op | source)
XLA Modules:
  0.0 100.2 jit_solution(593446089051910059)
XLA Ops:
  0.0 98.5 %block_backward.1 = bf16[128,768]{1,0:T(8,128)(2,1)} custom-call(bf16[8,16,768]{2,1,0:T(8,128)(2,1)} %bitcast.12, bf16[8,16,768]{2,1,0:T(8,128)(2,1)} %bitcast.13, bf16[576,768]{1,0:T(8,128)(2,1)} %bitcast.7, bf16[1,192,768]{2,1,0:T(8,128)(2,1)} %bitcast.9, bf16[3,192,768]{2,1,0:T(8,128)(2,1)} %wqv_in.1, bf16[1,192,768]{2,1,0:T(8,128)(2,1)} %bitcast.10, ...), custom_call_target="tpu_custom_call" | custom-call | tf_op jit(solution)/shard_map/block_backward/pallas_call | solution.py:469
  98.5 1.6 %copy.10 = bf16[1,1,128,768]{3,2,1,0:T(8,128)(2,1)} copy(bf16[1,1,128,768]{3,2,1,0:T(8,128)(2,1)} %bitcast.8) | data formatting | bytes 393216

commit v2 on v1

--- a/solution.py
+++ b/solution.py
@@ -94,6 +94,12 @@
     def plus(me, k, n):
         return lax.rem(me + k + n, n)
 
+    bits = [t % 2, t // 2 % 2, t // 4]
+
+    def paired(m):
+        return t + sum((1 - 2 * bits[at]) * 2**at for at in range(3) if m >> at & 1)
+
+    tm_order = (6, 7, 4, 5, 2, 3, 1)
     sent = []
     count = [0]
 
@@ -274,31 +280,22 @@
     g_qv.b()
     g_os.c()
     g_ov.a()
+    attend_space(1)
     g_ot.a()
-    attend_space(1)
     attend_space(3)
     g_qv.c()
     g_ov.b()
-    g_ot.b()
+    g_qt.a()
     attend_space(0)
     g_os.d()
-    g_qt.a()
     g_ov.c()
-    g_ot.c()
+    g_ot.b()
 
     def slot_of(view):
         return lax.rem(v - view + NV, NV)
 
-    c2_num = [ticket() for _ in range(NT_)]
-    for k in range(1, NV):
-        landed(c1.at[k], c1_num[k], "view", plus(v, -k, NV))
-    for j in range(1, NT_):
-        to = plus(t, j, NT_)
-        push(c1.at[slot_of(to)], c2.at[j], "tm", to, c2_num[j])
-    c2[0] = c1[slot_of(t)]
     g_qv.d()
     g_ov.d()
-    g_ot.d()
     g_os.e()
 
     for j in range(1, NV):
@@ -308,11 +305,18 @@
             if k or j:
                 group = plus(s, k, NSP)
                 landed(att.at[group, j], a_num[k][j], ("view", "space"), (plus(v, -j, NV), group))
+    c2_num = [ticket() for _ in range(NT_)]
+    for k in range(1, NV):
+        landed(c1.at[k], c1_num[k], "view", plus(v, -k, NV))
+    for m in tm_order:
+        push(c1.at[slot_of(paired(m))], c2.at[m], "tm", paired(m), c2_num[m])
+    c2[0] = c1[slot_of(t)]
+    g_ot.c()
+    g_qt.b()
     term = dot(att[0].reshape(TOK, LW), wos[0, :LW, :], NN)
     for h in range(1, NSP):
         term += dot(att[h].reshape(TOK, LW), wos[0, h * LW : (h + 1) * LW, :], NN)
     x2[...] = (xb[...].reshape(TOK, D).astype(F32) + term).astype(BF).reshape(NV, CH, D)
-    g_qt.b()
     rows_view = x2[...].reshape(TOK, D)
     normed, _ = rms(rows_view.astype(F32))
     tokens = normed.astype(BF)
@@ -346,43 +350,44 @@
         queries, key_t, value_t, shares = attend_small(wqv, g)
         qts_v[g], kt_v[g], vt_v[g], pt_v[g] = queries, key_t, value_t, shares
         outs.append(per_head(value_t, shares).astype(BF))
-        if g == 1:
+        if g == 0:
+            g_ot.d()
             g_qt.c()
     g_ov.e()
     term = dot(jnp.concatenate(outs, axis=0), wov[0], TN)
     xt[...] = (rows_view.astype(F32) + term).astype(BF).reshape(NV, CH, D)
 
     x3_num = [ticket() for _ in range(NT_)]
-    for j in range(1, NT_):
-        to = plus(t, j, NT_)
-        push(xt.at[slot_of(to)], x3.at[j], "tm", to, x3_num[j])
+    for m in tm_order:
+        push(xt.at[slot_of(paired(m))], x3.at[m], "tm", paired(m), x3_num[m])
     x3[0] = xt[slot_of(t)]
     g_qt.d()
-    for j in range(1, NT_):
-        landed(c2.at[j], c2_num[j], "tm", plus(t, -j, NT_))
-    for j in range(1, NT_):
-        landed(x3.at[j], x3_num[j], "tm", plus(t, -j, NT_))
+    g_ot.e()
+    for m in tm_order:
+        landed(c2.at[m], c2_num[m], "tm", paired(m))
+    upstream = c2[...].reshape(TOK, D)
+    out_grads = dot(wot[0], upstream, NT).astype(BF)
+    for m in tm_order:
+        landed(x3.at[m], x3_num[m], "tm", paired(m))
     rows_time = x3[...].reshape(TOK, D)
     normed, _ = rms(rows_time.astype(F32))
     tokens = normed.astype(BF)
-    upstream = c2[...].reshape(TOK, D)
     g_qt.e()
-    g_ot.e()
 
     total = jnp.zeros((TOK, D), F32)
     for g in range(GROUPS):
         queries, key_t, value_t, shares = attend_small(wqt, g)
-        out_grad = dot(wot[0, g * GW : (g + 1) * GW, :], upstream, NT).astype(BF)
+        out_grad = out_grads[g * GW : (g + 1) * GW]
         total += backward_small(wqt, g, queries, key_t, value_t, shares, out_grad)
     ut[...] = finish(upstream, rows_time, total).reshape(NT_, CH, D)
 
     u2_num = [ticket() for _ in range(NT_)]
     here = slot_of(t)
-    for j in range(1, NT_):
-        push(ut.at[j], u2.at[here], "tm", plus(t, -j, NT_), u2_num[j])
+    for m in tm_order:
+        push(ut.at[m], u2.at[here], "tm", paired(m), u2_num[m])
     u2[pl.ds(here, 1)] = ut[0:1]
-    for j in range(1, NT_):
-        landed(u2.at[slot_of(plus(t, j, NT_))], u2_num[j], "tm", plus(t, j, NT_))
+    for m in tm_order:
+        landed(u2.at[slot_of(paired(m))], u2_num[m], "tm", paired(m))
     upstream = u2[...].reshape(TOK, D)
     total = jnp.zeros((TOK, D), F32)
     for g in range(GROUPS):
@@ -402,11 +407,6 @@
             if k or j:
                 push(ogs.at[to[1], j], og.at[k, v], ("view", "space"), to, og_num[k][j])
     og[0:1, pl.ds(v, 1)] = ogs[pl.ds(s, 1), 0:1]
-    u3_num = [ticket() for _ in range(NV)]
-    for j in order:
-        push(uv.at[j], u3.at[v], "view", plus(v, -j, NV), u3_num[j])
-    u3[pl.ds(v, 1)] = uv[0:1]
-
     def backward_space(k):
         at = slice(k * LH * TOK, (k + 1) * LH * TOK)
         out_grad = og[k].reshape(TOK, LW)
@@ -421,12 +421,17 @@
 
     head_at = lax.broadcasted_iota(jnp.int32, (TOK, LW), 1) // HD
     nmask = [(head_at == h).astype(F32).astype(BF) for h in range(LH)]
+    u3_num = [ticket() for _ in range(NV)]
     for k in (0, 1, 3, 2):
         for j in range(NV):
             if k or j:
                 frm = (plus(v, j, NV), plus(s, -k, NSP))
                 landed(og.at[k, frm[0]], og_num[k][j], ("view", "space"), frm)
+        if k == 2:
+            for j in order:
+                push(uv.at[j], u3.at[v], "view", plus(v, -j, NV), u3_num[j])
         backward_space(k)
+    u3[pl.ds(v, 1)] = uv[0:1]
 
     def partial_sums(k):
         at = pl.ds(pl.multiple_of(k * TOK, TOK), TOK)

time: 101 us -> 101 us (level); the launches traced: 100 us -> 101 us
  Pallas kernels: 98.5 us -> 99.6 us
    pallas_call x1, Pallas kernels: 98.5 us -> 99.6 us  [on_device(): pl.pallas_call(body, out_shape=jax.ShapeDtypeStruct((TOK, D), BF), in_spe...]
where the time goes in v2:
time: 101 us
  Pallas kernels  99.6 us (99%)
  local copies, waits for them, and re-layouts  1.62 us (2%)
    pallas_call x1, Pallas kernels, on_device(): pl.pallas_call(body, out_shape=jax.ShapeDtypeStruct((TOK, D), BF), in_spe...  99.6 us

profile of v2, /device:TPU:2, one launch (start us, length us, event | category | flops | bytes accessed | tf_op | source)
XLA Modules:
  0.0 101.2 jit_solution(6044818761677590911)
XLA Ops:
  0.0 99.6 %block_backward.1 = bf16[128,768]{1,0:T(8,128)(2,1)} custom-call(bf16[8,16,768]{2,1,0:T(8,128)(2,1)} %bitcast.12, bf16[8,16,768]{2,1,0:T(8,128)(2,1)} %bitcast.13, bf16[576,768]{1,0:T(8,128)(2,1)} %bitcast.7, bf16[1,192,768]{2,1,0:T(8,128)(2,1)} %bitcast.9, bf16[3,192,768]{2,1,0:T(8,128)(2,1)} %wqv_in.1, bf16[1,192,768]{2,1,0:T(8,128)(2,1)} %bitcast.10, ...), custom_call_target="tpu_custom_call" | custom-call | tf_op jit(solution)/shard_map/block_backward/pallas_call | solution.py:474
  99.6 1.6 %copy.10 = bf16[1,1,128,768]{3,2,1,0:T(8,128)(2,1)} copy(bf16[1,1,128,768]{3,2,1,0:T(8,128)(2,1)} %bitcast.8) | data formatting | bytes 393216

commit v3 on v2

--- a/solution.py
+++ b/solution.py
@@ -21,9 +21,6 @@
 HD = 64
 LH = 3
 LW = LH * HD
-GH = 4
-GW = GH * HD
-GROUPS = D // GW
 SCALE = HD**-0.5
 NSEM = 208
 
@@ -170,16 +167,24 @@
             landed(part, self.x2, "space", s_prev)
             push(part, part, "view", y_next, self.ys[2])
 
-        def d(self):
-            for at in range(3):
+        def d(self, which):
+            for at in which:
                 landed(self.piece(self.others[at], core, 1 - half), self.ys[at], "view", y_next)
                 part = self.piece(self.others[at], core, 0, 96)
                 push(part, part, "tm", sibling, self.sib[at])
 
-        def e(self):
-            for at in range(3):
+        def ready(self, turn):
+            if turn == 0:
+                self.own.wait()
+            else:
+                at = turn - 1
                 landed(self.piece(self.others[at], 1 - core, 0, 96), self.sib[at], "tm", sibling)
-            self.own.wait()
+
+    NEAR, FAR = (0, 1), (2,)
+    turns = [s, plus(s, -1, 4), plus(s, 1, 4), plus(s, 2, 4)]
+
+    def group_rows(turn):
+        return pl.ds(pl.multiple_of(turns[turn] * LW, 16), LW)
 
     g_os = Gather(wos_in, wos, 0)
     g_qv = Gather(wqv_in, wqv, 1)
@@ -211,11 +216,10 @@
     x_rows = x_ref[...].reshape(TOK, D)
     normed, _ = rms(x_rows.astype(F32))
     nb[0] = normed.astype(BF)
-    key_at = lax.broadcasted_iota(jnp.int32, (TOK, GH * TOK), 0)
-    query_at = lax.broadcasted_iota(jnp.int32, (TOK, GH * TOK), 1)
+    key_at = lax.broadcasted_iota(jnp.int32, (TOK, LH * TOK), 0)
+    query_at = lax.broadcasted_iota(jnp.int32, (TOK, LH * TOK), 1)
     bias[...] = jnp.where(lax.rem(key_at, CH) == lax.rem(query_at, CH), 0.0, -1e30)
     lmask = head_masks(LW)
-    gmask = head_masks(GW)
     pl.semaphore_wait(barrier, NSP * NV + NT_ - 2)
 
     halves = [slice(0, TOK // 2), slice(TOK // 2, TOK)]
@@ -287,24 +291,24 @@
     g_ov.b()
     g_qt.a()
     attend_space(0)
-    g_os.d()
+    g_os.d(NEAR)
     g_ov.c()
     g_ot.b()
+    g_qv.d(NEAR)
+    g_os.d(FAR)
 
     def slot_of(view):
         return lax.rem(v - view + NV, NV)
 
-    g_qv.d()
-    g_ov.d()
-    g_os.e()
-
     for j in range(1, NV):
         landed(xb.at[j], x2_num[j], "view", plus(v, -j, NV))
-    for k in (2, 1, 3, 0):
+    total = xb[...].reshape(TOK, D).astype(F32)
+    for turn, k in enumerate((0, 3, 1, 2)):
         for j in range(NV):
             if k or j:
-                group = plus(s, k, NSP)
-                landed(att.at[group, j], a_num[k][j], ("view", "space"), (plus(v, -j, NV), group))
+                frm = (plus(v, -j, NV), plus(s, k, NSP))
+                landed(att.at[frm[1], j], a_num[k][j], ("view", "space"), frm)
+    g_qv.d(FAR)
     c2_num = [ticket() for _ in range(NT_)]
     for k in range(1, NV):
         landed(c1.at[k], c1_num[k], "view", plus(v, -k, NV))
@@ -313,27 +317,27 @@
     c2[0] = c1[slot_of(t)]
     g_ot.c()
     g_qt.b()
-    term = dot(att[0].reshape(TOK, LW), wos[0, :LW, :], NN)
-    for h in range(1, NSP):
-        term += dot(att[h].reshape(TOK, LW), wos[0, h * LW : (h + 1) * LW, :], NN)
-    x2[...] = (xb[...].reshape(TOK, D).astype(F32) + term).astype(BF).reshape(NV, CH, D)
+    for turn in range(NSP):
+        g_os.ready(turn)
+        total += dot(att[turns[turn]].reshape(TOK, LW), wos[0, group_rows(turn), :], NN)
+    x2[...] = total.astype(BF).reshape(NV, CH, D)
     rows_view = x2[...].reshape(TOK, D)
     normed, _ = rms(rows_view.astype(F32))
     tokens = normed.astype(BF)
-    g_qv.e()
-
-    def attend_small(w, g):
-        lanes = slice(g * GW, (g + 1) * GW)
-        query = dot(w[0, lanes, :], tokens, NT).astype(BF) * jnp.asarray(SCALE, BF)
-        key_t = dot(w[1, lanes, :], tokens, NT).astype(BF)
-        value_t = dot(w[2, lanes, :], tokens, NT).astype(BF)
-        queries = stacked(query, gmask)
+    g_ov.d(NEAR)
+
+    def attend_small(w, turn):
+        at = group_rows(turn)
+        query = dot(w[0, at, :], tokens, NT).astype(BF) * jnp.asarray(SCALE, BF)
+        key_t = dot(w[1, at, :], tokens, NT).astype(BF)
+        value_t = dot(w[2, at, :], tokens, NT).astype(BF)
+        queries = stacked(query, lmask)
         shares = softmax0(dot(key_t, queries, TN) + bias[...]).astype(BF)
         return queries, key_t, value_t, shares
 
-    def backward_small(w, g, queries, key_t, value_t, shares, out_grad):
-        lanes = slice(g * GW, (g + 1) * GW)
-        grads = stacked(out_grad, gmask)
+    def backward_small(w, turn, queries, key_t, value_t, shares, out_grad):
+        at = group_rows(turn)
+        grads = stacked(out_grad, lmask)
         share_grad = dot(value_t, grads, TN)
         wide = shares.astype(F32)
         row_dot = jnp.sum(wide * share_grad, axis=0, keepdims=True)
@@ -341,44 +345,50 @@
         query_grad = (per_head(key_t, score_grad) * SCALE).astype(BF)
         key_grad = dot(score_grad, queries, NT).astype(BF)
         value_grad = dot(shares, grads, NT).astype(BF)
-        total = dot(query_grad, w[0, lanes, :], TN)
-        total += dot(key_grad, w[1, lanes, :], NN)
-        return total + dot(value_grad, w[2, lanes, :], NN)
-
-    outs = []
-    for g in range(GROUPS):
-        queries, key_t, value_t, shares = attend_small(wqv, g)
-        qts_v[g], kt_v[g], vt_v[g], pt_v[g] = queries, key_t, value_t, shares
-        outs.append(per_head(value_t, shares).astype(BF))
-        if g == 0:
-            g_ot.d()
+        total = dot(query_grad, w[0, at, :], TN)
+        total += dot(key_grad, w[1, at, :], NN)
+        return total + dot(value_grad, w[2, at, :], NN)
+
+    total = rows_view.astype(F32)
+    for turn in range(NSP):
+        g_qv.ready(turn)
+        queries, key_t, value_t, shares = attend_small(wqv, turn)
+        qts_v[turn], kt_v[turn], vt_v[turn], pt_v[turn] = queries, key_t, value_t, shares
+        out = per_head(value_t, shares).astype(BF)
+        g_ov.ready(turn)
+        total += dot(out, wov[0, group_rows(turn), :], TN)
+        if turn == 0:
+            g_ov.d(FAR)
+            g_ot.d(NEAR)
+        if turn == 1:
             g_qt.c()
-    g_ov.e()
-    term = dot(jnp.concatenate(outs, axis=0), wov[0], TN)
-    xt[...] = (rows_view.astype(F32) + term).astype(BF).reshape(NV, CH, D)
+            g_ot.d(FAR)
+        if turn == 2:
+            g_qt.d(NEAR)
+    xt[...] = total.astype(BF).reshape(NV, CH, D)
 
     x3_num = [ticket() for _ in range(NT_)]
     for m in tm_order:
         push(xt.at[slot_of(paired(m))], x3.at[m], "tm", paired(m), x3_num[m])
     x3[0] = xt[slot_of(t)]
-    g_qt.d()
-    g_ot.e()
+    g_qt.d(FAR)
     for m in tm_order:
         landed(c2.at[m], c2_num[m], "tm", paired(m))
     upstream = c2[...].reshape(TOK, D)
-    out_grads = dot(wot[0], upstream, NT).astype(BF)
+    out_grads = []
+    for turn in range(NSP):
+        g_ot.ready(turn)
+        out_grads.append(dot(wot[0, group_rows(turn), :], upstream, NT).astype(BF))
     for m in tm_order:
         landed(x3.at[m], x3_num[m], "tm", paired(m))
     rows_time = x3[...].reshape(TOK, D)
     normed, _ = rms(rows_time.astype(F32))
     tokens = normed.astype(BF)
-    g_qt.e()
 
     total = jnp.zeros((TOK, D), F32)
-    for g in range(GROUPS):
-        queries, key_t, value_t, shares = attend_small(wqt, g)
-        out_grad = out_grads[g * GW : (g + 1) * GW]
-        total += backward_small(wqt, g, queries, key_t, value_t, shares, out_grad)
+    for turn in range(NSP):
+        g_qt.ready(turn)
+        total += backward_small(wqt, turn, *attend_small(wqt, turn), out_grads[turn])
     ut[...] = finish(upstream, rows_time, total).reshape(NT_, CH, D)
 
     u2_num = [ticket() for _ in range(NT_)]
@@ -390,9 +400,10 @@
         landed(u2.at[slot_of(paired(m))], u2_num[m], "tm", paired(m))
     upstream = u2[...].reshape(TOK, D)
     total = jnp.zeros((TOK, D), F32)
-    for g in range(GROUPS):
-        out_grad = dot(wov[0, g * GW : (g + 1) * GW, :], upstream, NT).astype(BF)
-        total += backward_small(wqv, g, qts_v[g], kt_v[g], vt_v[g], pt_v[g], out_grad)
+    for turn in range(NSP):
+        out_grad = dot(wov[0, group_rows(turn), :], upstream, NT).astype(BF)
+        saved = (qts_v[turn], kt_v[turn], vt_v[turn], pt_v[turn])
+        total += backward_small(wqv, turn, *saved, out_grad)
     upstream = finish(upstream, x2[...].reshape(TOK, D), total)
     uv[...] = upstream.reshape(NV, CH, D)
 
@@ -499,11 +510,11 @@
             buf(3, TOK, D),
             buf(2, TOK, D),
             buf(TOK, D),
-            buf(TOK, GH * TOK, dtype=F32),
-            buf(GROUPS, GW, TOK),
-            buf(GROUPS, GW, TOK),
-            buf(GROUPS, GW, GH * TOK),
-            buf(GROUPS, TOK, GH * TOK),
+            buf(TOK, LH * TOK, dtype=F32),
+            buf(NSP, LW, TOK),
+            buf(NSP, LW, TOK),
+            buf(NSP, LW, LH * TOK),
+            buf(NSP, TOK, LH * TOK),
             buf(1, D, D),
             buf(3, D, D),
             buf(1, D, D),

time: 101 us -> 104 us (1.030); the launches traced: 101 us -> 102 us
  no operation moved by 1% of the time
where the time goes in v3:
time: 104 us; the launch traced here: 102 us
  Pallas kernels  100 us (96%)
  local copies, waits for them, and re-layouts  1.62 us (2%)
    pallas_call x1, Pallas kernels, on_device(): pl.pallas_call(body, out_shape=jax.ShapeDtypeStruct((TOK, D), BF), in_spe...  100 us

profile of v3, /device:TPU:2, one launch (start us, length us, event | category | flops | bytes accessed | tf_op | source)
XLA Modules:
  0.0 101.9 jit_solution(2986784475475817751)
XLA Ops:
  0.0 100.3 %block_backward.1 = bf16[128,768]{1,0:T(8,128)(2,1)} custom-call(bf16[8,16,768]{2,1,0:T(8,128)(2,1)} %bitcast.12, bf16[8,16,768]{2,1,0:T(8,128)(2,1)} %bitcast.13, bf16[576,768]{1,0:T(8,128)(2,1)} %bitcast.7, bf16[1,192,768]{2,1,0:T(8,128)(2,1)} %bitcast.9, bf16[3,192,768]{2,1,0:T(8,128)(2,1)} %wqv_in.1, bf16[1,192,768]{2,1,0:T(8,128)(2,1)} %bitcast.10, ...), custom_call_target="tpu_custom_call" | custom-call | tf_op jit(solution)/shard_map/block_backward/pallas_call | solution.py:485
  100.3 1.6 %copy.10 = bf16[1,1,128,768]{3,2,1,0:T(8,128)(2,1)} copy(bf16[1,1,128,768]{3,2,1,0:T(8,128)(2,1)} %bitcast.8) | data formatting | bytes 393216

commit v4 on v2

--- a/solution.py
+++ b/solution.py
@@ -25,7 +25,7 @@
 GW = GH * HD
 GROUPS = D // GW
 SCALE = HD**-0.5
-NSEM = 208
+NSEM = 64
 
 
 def dot(a, b, dims):
@@ -72,11 +72,11 @@
 def body(
     x_in, cot_in, wqs_in, wos_in, wqv_in, wov_in, wqt_in, wot_in,
     out_ref,
-    x_ref, cot_ref, wqs_ref,
+    xc, wqs_ref,
     nb, k_nat, v_nat, qts, kvt, pts, gts, ogts, dqt, ats, att,
-    xb, x2, xt, x3, c1, c2, ut, u2, uv, u3, ogs, og, rsend, rs, rf,
+    xb, x2, xt, x3, c2, ut, u2, uv, u3, ogs, og, rsend, rs, rf,
     bias, kt_v, vt_v, qts_v, pt_v,
-    wos, wqv, wov, wqt, wot,
+    whole,
     send_sem, recv_sem, local_sem,
 ):
     t = lax.axis_index("tm")
@@ -100,96 +100,98 @@
         return t + sum((1 - 2 * bits[at]) * 2**at for at in range(3) if m >> at & 1)
 
     tm_order = (6, 7, 4, 5, 2, 3, 1)
-    sent = []
+    left = []
     count = [0]
 
     def ticket():
         count[0] += 1
         return count[0] - 1
 
-    def push(src, dst, axis, index, number):
+    def remote(src, dst, axis, index, number, arrival):
         to = {axis: index} if isinstance(axis, str) else dict(zip(axis, index))
-        copy = pltpu.make_async_remote_copy(
+        return pltpu.make_async_remote_copy(
             src_ref=src,
             dst_ref=dst,
             send_sem=send_sem.at[number],
-            recv_sem=recv_sem.at[number],
+            recv_sem=recv_sem.at[arrival],
             device_id=to,
             device_id_type=MESH,
         )
-        copy.start()
-        sent.append(copy)
-
-    def landed(dst, number, axis, index):
-        to = {axis: index} if isinstance(axis, str) else dict(zip(axis, index))
-        pltpu.make_async_remote_copy(
-            src_ref=dst,
-            dst_ref=dst,
-            send_sem=send_sem.at[number],
-            recv_sem=recv_sem.at[number],
-            device_id=to,
-            device_id_type=MESH,
-        ).wait_recv()
+
+    def push(src, dst, axis, index, number, arrival):
+        remote(src, dst, axis, index, number, arrival).start()
+
+    def landed(ref, arrival):
+        remote(ref, ref, "tm", sibling, 0, arrival).wait_recv()
+
+    def sending(ref):
+        left.append((ref, ticket()))
+        return left[-1][1]
 
     def rows(owner, c, h, size):
         return pl.ds(pl.multiple_of(owner * LW + c * 96 + h * 48, 16), size)
 
     class Gather:
-        def __init__(self, shard, full, number):
-            self.shard, self.full = shard, full
-            self.x1 = [ticket(), ticket()]
-            self.x2 = ticket()
-            self.ys = [ticket() for _ in range(3)]
-            self.sib = [ticket() for _ in range(3)]
+        def __init__(self, first, end):
+            self.first, self.end = first, end
             self.others = [plus(s, -1, 4), plus(s, 1, 4), plus(s, 2, 4)]
-            self.own = pltpu.make_async_copy(
-                shard, full.at[:, pl.ds(pl.multiple_of(s * LW, 16), LW), :], local_sem.at[number]
-            )
+            self.out = [sending(self.bytes_of(size)) for size in (96, 48, 144, 288)]
+            self.near, self.far, self.y_near, self.y_far, self.sib = [ticket() for _ in range(5)]
+
+        def bytes_of(self, size):
+            return whole.at[self.first : self.end, 0:size, :]
 
         def piece(self, owner, c, h, size=48):
-            return self.full.at[:, rows(owner, c, h, size), :]
+            return whole.at[self.first : self.end, rows(owner, c, h, size), :]
 
         def a(self):
-            self.own.start()
-            mine = self.shard.at[:, pl.ds(pl.multiple_of(core * 96 + half * 48, 16), 48), :]
-            there = self.piece(s, core, half)
-            push(mine, there, "space", plus(s, 1, 4), self.x1[0])
-            push(mine, there, "space", plus(s, -1, 4), self.x1[1])
+            mine = self.piece(s, core, half)
+            push(mine, mine, "space", plus(s, 1, 4), self.out[0], self.near)
+            push(mine, mine, "space", plus(s, -1, 4), self.out[0], self.near)
 
         def b(self):
-            for at in range(2):
-                landed(self.piece(self.others[at], core, half), self.x1[at], "space", self.others[at])
+            landed(self.bytes_of(96), self.near)
             far = self.piece(s_prev, core, half)
-            push(far, far, "space", s_next, self.x2)
+            push(far, far, "space", s_next, self.out[1], self.far)
             for at in range(2):
                 part = self.piece(self.others[at], core, half)
-                push(part, part, "view", y_next, self.ys[at])
+                push(part, part, "view", y_next, self.out[2], self.y_near)
 
         def c(self):
+            landed(self.bytes_of(48), self.far)
             part = self.piece(self.others[2], core, half)
-            landed(part, self.x2, "space", s_prev)
-            push(part, part, "view", y_next, self.ys[2])
+            push(part, part, "view", y_next, self.out[2], self.y_far)
 
         def d(self):
+            landed(self.bytes_of(96), self.y_near)
             for at in range(3):
-                landed(self.piece(self.others[at], core, 1 - half), self.ys[at], "view", y_next)
+                if at == 2:
+                    landed(self.bytes_of(48), self.y_far)
                 part = self.piece(self.others[at], core, 0, 96)
-                push(part, part, "tm", sibling, self.sib[at])
+                push(part, part, "tm", sibling, self.out[3], self.sib)
 
         def e(self):
-            for at in range(3):
-                landed(self.piece(self.others[at], 1 - core, 0, 96), self.sib[at], "tm", sibling)
-            self.own.wait()
-
-    g_os = Gather(wos_in, wos, 0)
-    g_qv = Gather(wqv_in, wqv, 1)
-    g_ov = Gather(wov_in, wov, 2)
-    g_qt = Gather(wqt_in, wqt, 3)
-    g_ot = Gather(wot_in, wot, 4)
+            landed(self.bytes_of(288), self.sib)
+
+    g_a, g_b, g_c = Gather(0, 4), Gather(4, 6), Gather(6, 9)
+    wos, wqv, wov = whole.at[0:1], whole.at[1:4], whole.at[4:5]
+    wot, wqt = whole.at[5:6], whole.at[6:9]
+    own = pl.ds(pl.multiple_of(s * LW, 16), LW)
 
     loads = [
-        pltpu.make_async_copy(src, dst, local_sem.at[5 + at])
-        for at, (src, dst) in enumerate(((x_in, x_ref), (wqs_in, wqs_ref), (cot_in, cot_ref)))
+        pltpu.make_async_copy(src, dst, local_sem.at[at])
+        for at, (src, dst) in enumerate(
+            (
+                (x_in, xc.at[:, 0]),
+                (wqs_in, wqs_ref),
+                (cot_in, xc.at[:, 1]),
+                (wos_in, wos.at[:, own, :]),
+                (wqv_in, wqv.at[:, own, :]),
+                (wov_in, wov.at[:, own, :]),
+                (wot_in, wot.at[:, own, :]),
+                (wqt_in, wqt.at[:, own, :]),
+            )
+        )
     ]
     for copy in loads:
         copy.start()
@@ -208,7 +210,7 @@
         pl.semaphore_signal(barrier, inc=1, device_id={"tm": plus(t, k, NT_)}, device_id_type=MESH)
 
     loads[0].wait()
-    x_rows = x_ref[...].reshape(TOK, D)
+    x_rows = xc[:, 0].reshape(TOK, D)
     normed, _ = rms(x_rows.astype(F32))
     nb[0] = normed.astype(BF)
     key_at = lax.broadcasted_iota(jnp.int32, (TOK, GH * TOK), 0)
@@ -219,24 +221,19 @@
     pl.semaphore_wait(barrier, NSP * NV + NT_ - 2)
 
     halves = [slice(0, TOK // 2), slice(TOK // 2, TOK)]
-    n_num = [{k: ticket() for k in range(1, NSP)} for _ in halves]
+    n_near, n_far = [ticket() for _ in halves], [ticket() for _ in halves]
+    n_out = sending(nb.at[0:2]), sending(nb.at[0])
     for h, part in enumerate(halves):
         for k in (1, 3):
-            push(nb.at[0, part], nb.at[k, part], "space", plus(s, k, NSP), n_num[h][k])
-    loads[1].wait()
-    loads[2].wait()
-    g_os.a()
+            push(nb.at[0, part], nb.at[k, part], "space", plus(s, k, NSP), n_out[0], n_near[h])
+    for copy in loads[1:]:
+        copy.wait()
     order = (4, 3, 5, 2, 6, 1, 7)
-    x2_num = [ticket() for _ in range(NV)]
-    c1_num = [ticket() for _ in range(NV)]
+    x2_num, x2_out = ticket(), sending(xb.at[1:NV])
     for j in order:
         to = plus(v, j, NV)
-        push(x_ref.at[to], xb.at[j], "view", to, x2_num[j])
-    for j in order:
-        to = plus(v, j, NV)
-        push(cot_ref.at[to], c1.at[j], "view", to, c1_num[j])
-    xb[0] = x_ref[v]
-    c1[0] = cot_ref[v]
+        push(xc.at[to], xb.at[j], "view", to, x2_out, x2_num)
+    xb[0] = xc[v]
 
     def project_space(k):
         tokens = nb[k]
@@ -250,18 +247,17 @@
 
     project_space(0)
     for h, part in enumerate(halves):
-        for k in (1, 3):
-            landed(nb.at[k, part], n_num[h][k], "space", plus(s, -k, NSP))
-        push(nb.at[1 + 2 * core, part], nb.at[2, part], "space", s_next, n_num[h][2])
-    g_qv.a()
+        landed(nb.at[0], n_near[h])
+        push(nb.at[1 + 2 * core, part], nb.at[2, part], "space", s_next, n_out[1], n_far[h])
+    g_a.a()
     project_space(1)
     project_space(3)
-    g_os.b()
     for h, part in enumerate(halves):
-        landed(nb.at[2, part], n_num[h][2], "space", plus(s, 2, NSP))
+        landed(nb.at[2, part], n_far[h])
     project_space(2)
 
-    a_num = [[ticket() for _ in range(NV)] for _ in range(NSP)]
+    a_num = [ticket() for _ in range(NSP)]
+    a_out = sending(ats.at[0, 1:NV]), sending(ats.at[1:NSP])
 
     def attend_space(k):
         at = slice(k * LH * TOK, (k + 1) * LH * TOK)
@@ -272,55 +268,43 @@
         for j in order + (0,):
             to = (plus(v, j, NV), plus(s, -k, NSP))
             if k or j:
-                push(ats.at[k, to[0]], att.at[s, j], ("view", "space"), to, a_num[k][j])
+                push(ats.at[k, to[0]], att.at[s, j], ("view", "space"), to, a_out[min(k, 1)], a_num[k])
             else:
                 att[pl.ds(s, 1), 0:1] = ats[0:1, pl.ds(v, 1)]
 
     attend_space(2)
-    g_qv.b()
-    g_os.c()
-    g_ov.a()
+    g_a.b()
+    g_b.a()
     attend_space(1)
-    g_ot.a()
     attend_space(3)
-    g_qv.c()
-    g_ov.b()
-    g_qt.a()
+    g_a.c()
+    g_b.b()
+    g_c.a()
     attend_space(0)
-    g_os.d()
-    g_ov.c()
-    g_ot.b()
+    g_b.c()
+    g_a.d()
 
     def slot_of(view):
         return lax.rem(v - view + NV, NV)
 
-    g_qv.d()
-    g_ov.d()
-    g_os.e()
-
-    for j in range(1, NV):
-        landed(xb.at[j], x2_num[j], "view", plus(v, -j, NV))
-    for k in (2, 1, 3, 0):
-        for j in range(NV):
-            if k or j:
-                group = plus(s, k, NSP)
-                landed(att.at[group, j], a_num[k][j], ("view", "space"), (plus(v, -j, NV), group))
-    c2_num = [ticket() for _ in range(NT_)]
-    for k in range(1, NV):
-        landed(c1.at[k], c1_num[k], "view", plus(v, -k, NV))
+    g_b.d()
+    landed(xb.at[1:NV], x2_num)
+    for k in (2, 1, 3):
+        landed(att.at[plus(s, k, NSP)], a_num[k])
+    landed(att.at[s, 1:NV], a_num[0])
+    c2_num, c2_out = ticket(), sending(c2.at[1:NT_])
     for m in tm_order:
-        push(c1.at[slot_of(paired(m))], c2.at[m], "tm", paired(m), c2_num[m])
-    c2[0] = c1[slot_of(t)]
-    g_ot.c()
-    g_qt.b()
+        push(xb.at[slot_of(paired(m)), 1], c2.at[m], "tm", paired(m), c2_out, c2_num)
+    c2[0] = xb[slot_of(t), 1]
+    g_c.b()
+    g_a.e()
     term = dot(att[0].reshape(TOK, LW), wos[0, :LW, :], NN)
     for h in range(1, NSP):
         term += dot(att[h].reshape(TOK, LW), wos[0, h * LW : (h + 1) * LW, :], NN)
-    x2[...] = (xb[...].reshape(TOK, D).astype(F32) + term).astype(BF).reshape(NV, CH, D)
+    x2[...] = (xb[:, 0].reshape(TOK, D).astype(F32) + term).astype(BF).reshape(NV, CH, D)
     rows_view = x2[...].reshape(TOK, D)
     normed, _ = rms(rows_view.astype(F32))
     tokens = normed.astype(BF)
-    g_qv.e()
 
     def attend_small(w, g):
         lanes = slice(g * GW, (g + 1) * GW)
@@ -351,28 +335,24 @@
         qts_v[g], kt_v[g], vt_v[g], pt_v[g] = queries, key_t, value_t, shares
         outs.append(per_head(value_t, shares).astype(BF))
         if g == 0:
-            g_ot.d()
-            g_qt.c()
-    g_ov.e()
+            g_c.c()
+    g_b.e()
     term = dot(jnp.concatenate(outs, axis=0), wov[0], TN)
     xt[...] = (rows_view.astype(F32) + term).astype(BF).reshape(NV, CH, D)
 
-    x3_num = [ticket() for _ in range(NT_)]
+    x3_num, x3_out = ticket(), sending(x3.at[1:NT_])
     for m in tm_order:
-        push(xt.at[slot_of(paired(m))], x3.at[m], "tm", paired(m), x3_num[m])
+        push(xt.at[slot_of(paired(m))], x3.at[m], "tm", paired(m), x3_out, x3_num)
     x3[0] = xt[slot_of(t)]
-    g_qt.d()
-    g_ot.e()
-    for m in tm_order:
-        landed(c2.at[m], c2_num[m], "tm", paired(m))
+    g_c.d()
+    landed(c2.at[1:NT_], c2_num)
     upstream = c2[...].reshape(TOK, D)
     out_grads = dot(wot[0], upstream, NT).astype(BF)
-    for m in tm_order:
-        landed(x3.at[m], x3_num[m], "tm", paired(m))
+    landed(x3.at[1:NT_], x3_num)
+    g_c.e()
     rows_time = x3[...].reshape(TOK, D)
     normed, _ = rms(rows_time.astype(F32))
     tokens = normed.astype(BF)
-    g_qt.e()
 
     total = jnp.zeros((TOK, D), F32)
     for g in range(GROUPS):
@@ -381,13 +361,12 @@
         total += backward_small(wqt, g, queries, key_t, value_t, shares, out_grad)
     ut[...] = finish(upstream, rows_time, total).reshape(NT_, CH, D)
 
-    u2_num = [ticket() for _ in range(NT_)]
+    u2_num, u2_out = ticket(), sending(ut.at[1:NT_])
     here = slot_of(t)
     for m in tm_order:
-        push(ut.at[m], u2.at[here], "tm", paired(m), u2_num[m])
+        push(ut.at[m], u2.at[here], "tm", paired(m), u2_out, u2_num)
     u2[pl.ds(here, 1)] = ut[0:1]
-    for m in tm_order:
-        landed(u2.at[slot_of(paired(m))], u2_num[m], "tm", paired(m))
+    landed(u2.at[1:NT_], u2_num)
     upstream = u2[...].reshape(TOK, D)
     total = jnp.zeros((TOK, D), F32)
     for g in range(GROUPS):
@@ -400,12 +379,13 @@
     for h in range(NSP):
         part = jnp.transpose(out_grad[h * LW : (h + 1) * LW]).astype(BF)
         ogs[h] = part.reshape(NV, CH, LW)
-    og_num = [[ticket() for _ in range(NV)] for _ in range(NSP)]
+    og_num = [ticket() for _ in range(NSP)]
+    og_out = sending(ogs.at[0, 1:NV]), sending(ogs.at[1:NSP])
     for k in (2, 1, 3, 0):
         for j in order + (0,):
             to = (plus(v, -j, NV), plus(s, k, NSP))
             if k or j:
-                push(ogs.at[to[1], j], og.at[k, v], ("view", "space"), to, og_num[k][j])
+                push(ogs.at[to[1], j], og.at[k, v], ("view", "space"), to, og_out[min(k, 1)], og_num[k])
     og[0:1, pl.ds(v, 1)] = ogs[pl.ds(s, 1), 0:1]
     def backward_space(k):
         at = slice(k * LH * TOK, (k + 1) * LH * TOK)
@@ -421,15 +401,12 @@
 
     head_at = lax.broadcasted_iota(jnp.int32, (TOK, LW), 1) // HD
     nmask = [(head_at == h).astype(F32).astype(BF) for h in range(LH)]
-    u3_num = [ticket() for _ in range(NV)]
+    u3_num, u3_out = ticket(), sending(uv.at[1:NV])
     for k in (0, 1, 3, 2):
-        for j in range(NV):
-            if k or j:
-                frm = (plus(v, j, NV), plus(s, -k, NSP))
-                landed(og.at[k, frm[0]], og_num[k][j], ("view", "space"), frm)
+        landed(og.at[k] if k else og.at[0, 1:NV], og_num[k])
         if k == 2:
             for j in order:
-                push(uv.at[j], u3.at[v], "view", plus(v, -j, NV), u3_num[j])
+                push(uv.at[j], u3.at[v], "view", plus(v, -j, NV), u3_out, u3_num)
         backward_space(k)
     u3[pl.ds(v, 1)] = uv[0:1]
 
@@ -442,25 +419,25 @@
         return part + dot(value_grad, wqs_ref[2 * LW :, :], NN)
 
     rf_num, near_num, late_num = ticket(), ticket(), ticket()
+    rs_out = sending(rsend)
     rsend[0] = partial_sums(2).astype(BF)
-    push(rsend.at[0], rf, "space", s_next, rf_num)
+    push(rsend.at[0], rf, "space", s_next, rs_out, rf_num)
     rsend[1] = partial_sums(1 + 2 * core).astype(BF)
-    push(rsend.at[1], rs.at[0], "space", s_prev, near_num)
+    push(rsend.at[1], rs.at[0], "space", s_prev, rs_out, near_num)
     late = partial_sums(3 - 2 * core)
-    landed(rf, rf_num, "space", s_prev)
+    landed(rf, rf_num)
     rsend[2] = (late + rf[...].astype(F32)).astype(BF)
-    push(rsend.at[2], rs.at[1], "space", s_next, late_num)
+    push(rsend.at[2], rs.at[1], "space", s_next, rs_out, late_num)
     total = partial_sums(0)
-    landed(rs.at[0], near_num, "space", s_next)
+    landed(rs.at[0], near_num)
     total += rs[0].astype(F32)
-    landed(rs.at[1], late_num, "space", s_prev)
+    landed(rs.at[1], late_num)
     total += rs[1].astype(F32)
-    for j in range(1, NV):
-        landed(u3.at[plus(v, j, NV)], u3_num[j], "view", plus(v, j, NV))
-    out_ref[...] = finish(u3[...].reshape(TOK, D), x_ref[...].reshape(TOK, D), total)
-
-    for copy in sent:
-        copy.wait_send()
+    landed(u3.at[1:NV], u3_num)
+    out_ref[...] = finish(u3[...].reshape(TOK, D), xc[:, 0].reshape(TOK, D), total)
+
+    for ref, number in left:
+        remote(ref, ref, "tm", sibling, number, 0).wait_send()
 
 
 def on_device(latents, cotangent, wqs, wos, wqv, wov, wqt, wot):
@@ -477,8 +454,7 @@
         in_specs=[hbm] * 8,
         out_specs=vmem,
         scratch_shapes=[
-            buf(NV, CH, D),
-            buf(NV, CH, D),
+            buf(NV, 2, CH, D),
             buf(3 * LW, D),
             buf(NSP, TOK, D),
             buf(NSP * TOK, LW),
@@ -492,7 +468,8 @@
             buf(NSP, NV, CH, LW),
             buf(NSP, NV, CH, LW),
         ]
-        + [buf(NV, CH, D)] * 10
+        + [buf(NV, 2, CH, D)]
+        + [buf(NV, CH, D)] * 8
         + [
             buf(NSP, NV, CH, LW),
             buf(NSP, NV, CH, LW),
@@ -504,11 +481,7 @@
             buf(GROUPS, GW, TOK),
             buf(GROUPS, GW, GH * TOK),
             buf(GROUPS, TOK, GH * TOK),
-            buf(1, D, D),
-            buf(3, D, D),
-            buf(1, D, D),
-            buf(3, D, D),
-            buf(1, D, D),
+            buf(9, D, D),
             pltpu.SemaphoreType.DMA((NSEM,)),
             pltpu.SemaphoreType.DMA((NSEM,)),
             pltpu.SemaphoreType.DMA((8,)),

time: 101 us -> 99.9 us (0.989)
  Pallas kernels: 99.6 us -> 98.1 us
    pallas_call x1, Pallas kernels: 99.6 us -> 98.1 us  [on_device(): pl.pallas_call(body, out_shape=jax.ShapeDtypeStruct((TOK, D), BF), in_spe...]
where the time goes in v4:
time: 99.9 us; the launch traced here: 99.8 us
  Pallas kernels  98.1 us (98%)
  local copies, waits for them, and re-layouts  1.62 us (2%)
    pallas_call x1, Pallas kernels, on_device(): pl.pallas_call(body, out_shape=jax.ShapeDtypeStruct((TOK, D), BF), in_spe...  98.1 us

profile of v4, /device:TPU:2, one launch (start us, length us, event | category | flops | bytes accessed | tf_op | source)
XLA Modules:
  0.0 99.8 jit_solution(9232137569385259050)
XLA Ops:
  0.0 98.1 %block_backward.1 = bf16[128,768]{1,0:T(8,128)(2,1)} custom-call(bf16[8,16,768]{2,1,0:T(8,128)(2,1)} %bitcast.12, bf16[8,16,768]{2,1,0:T(8,128)(2,1)} %bitcast.13, bf16[576,768]{1,0:T(8,128)(2,1)} %bitcast.7, bf16[1,192,768]{2,1,0:T(8,128)(2,1)} %bitcast.9, bf16[3,192,768]{2,1,0:T(8,128)(2,1)} %wqv_in.1, bf16[1,192,768]{2,1,0:T(8,128)(2,1)} %bitcast.10, ...), custom_call_target="tpu_custom_call" | custom-call | tf_op jit(solution)/shard_map/block_backward/pallas_call | solution.py:451
  98.1 1.6 %copy.10 = bf16[1,1,128,768]{3,2,1,0:T(8,128)(2,1)} copy(bf16[1,1,128,768]{3,2,1,0:T(8,128)(2,1)} %bitcast.8) | data formatting | bytes 393216

commit v5 on v4

--- a/solution.py
+++ b/solution.py
@@ -94,12 +94,26 @@
     def plus(me, k, n):
         return lax.rem(me + k + n, n)
 
-    bits = [t % 2, t // 2 % 2, t // 4]
-
-    def paired(m):
-        return t + sum((1 - 2 * bits[at]) * 2**at for at in range(3) if m >> at & 1)
-
-    tm_order = (6, 7, 4, 5, 2, 3, 1)
+    z_hi, z_lo = v // 4, t // 2
+    even_odd = z_lo % 2
+    pair_z, pair_y = 2 * z_hi + z_lo // 2, y // 2
+    piece = 2 * pair_z + pair_y
+    frame = 4 * half + 2 * even_odd + core
+    apart = jnp.abs(half - z_lo // 2)
+
+    def home(dz, dy):
+        at_z, at_y = lax.rem(pair_z + dz, 4), lax.rem(pair_y + dy, 2)
+        to_tm = 2 * (2 * (at_z % 2) + even_odd) + core
+        to_view = 4 * (at_z // 2) + 2 * at_y + z_lo // 2
+        return 2 * at_z + at_y, to_tm, to_view
+
+    homes = ((2, 0), (2, 1), (1, 0), (3, 0), (1, 1), (3, 1), (0, 1), (0, 0))
+
+    def member(m):
+        flips = (1 - 2 * core) * (m & 1), (1 - 2 * even_odd) * (m >> 1 & 1), (1 - 2 * half) * (m >> 2)
+        return (t + flips[0] + 2 * flips[1], v + flips[2]), frame + flips[0] + 2 * flips[1] + 4 * flips[2]
+
+    members = (6, 7, 4, 5, 2, 3, 1)
     left = []
     count = [0]
 
@@ -124,8 +138,15 @@
     def landed(ref, arrival):
         remote(ref, ref, "tm", sibling, 0, arrival).wait_recv()
 
-    def sending(ref):
-        left.append((ref, ticket()))
+    def unless_alone(copies, here):
+        pl.when(apart == 1)(copies)
+        pl.when(apart == 0)(here)
+
+    def landed_all(ref, arrival):
+        unless_alone(lambda: landed(ref, arrival), lambda: landed(ref.at[1:], arrival))
+
+    def sending(ref, eight=False):
+        left.append((ref, ticket(), eight))
         return left[-1][1]
 
     def rows(owner, c, h, size):
@@ -197,18 +218,24 @@
         copy.start()
 
     barrier = pltpu.get_barrier_semaphore()
+    def greet(**to):
+        pl.semaphore_signal(barrier, inc=1, device_id=to, device_id_type=MESH)
+
     for k in range(NSP):
         for j in range(NV):
             if k or j:
-                pl.semaphore_signal(
-                    barrier,
-                    inc=1,
-                    device_id={"view": plus(v, j, NV), "space": plus(s, k, NSP)},
-                    device_id_type=MESH,
-                )
-    for k in range(1, NT_):
-        pl.semaphore_signal(barrier, inc=1, device_id={"tm": plus(t, k, NT_)}, device_id_type=MESH)
-
+                greet(tm=frame, view=plus(v, j, NV), space=plus(s, k, NSP))
+
+    @pl.when(apart == 1)
+    def _():
+        greet(tm=frame, view=v)
+
+    for m in members:
+        to = member(m)[0]
+        greet(tm=to[0], view=to[1])
+    greet(space=plus(s, 1, NSP))
+    greet(space=plus(s, -1, NSP))
+    greet(view=v - y + lax.rem(y - step + 4, 4))
     loads[0].wait()
     x_rows = xc[:, 0].reshape(TOK, D)
     normed, _ = rms(x_rows.astype(F32))
@@ -218,7 +245,7 @@
     bias[...] = jnp.where(lax.rem(key_at, CH) == lax.rem(query_at, CH), 0.0, -1e30)
     lmask = head_masks(LW)
     gmask = head_masks(GW)
-    pl.semaphore_wait(barrier, NSP * NV + NT_ - 2)
+    pl.semaphore_wait(barrier, NSP * NV - 1 + NT_ - 1 + 3 + apart)
 
     halves = [slice(0, TOK // 2), slice(TOK // 2, TOK)]
     n_near, n_far = [ticket() for _ in halves], [ticket() for _ in halves]
@@ -229,11 +256,19 @@
     for copy in loads[1:]:
         copy.wait()
     order = (4, 3, 5, 2, 6, 1, 7)
-    x2_num, x2_out = ticket(), sending(xb.at[1:NV])
-    for j in order:
-        to = plus(v, j, NV)
-        push(xc.at[to], xb.at[j], "view", to, x2_out, x2_num)
-    xb[0] = xc[v]
+    x2_num, x2_out = ticket(), sending(xb, True)
+
+    def send_tokens(dz, dy):
+        place, *to = home(dz, dy)
+        push(xc.at[place], xb.at[v], ("tm", "view"), to, x2_out, x2_num)
+
+    for dz, dy in homes[:-1]:
+        send_tokens(dz, dy)
+
+    def keep_tokens():
+        xb[pl.ds(v, 1)] = xc[pl.ds(piece, 1)]
+
+    unless_alone(lambda: send_tokens(0, 0), keep_tokens)
 
     def project_space(k):
         tokens = nb[k]
@@ -257,7 +292,7 @@
     project_space(2)
 
     a_num = [ticket() for _ in range(NSP)]
-    a_out = sending(ats.at[0, 1:NV]), sending(ats.at[1:NSP])
+    a_out = sending(ats.at[0], True), sending(ats.at[1:NSP])
 
     def attend_space(k):
         at = slice(k * LH * TOK, (k + 1) * LH * TOK)
@@ -265,12 +300,22 @@
         pts[:, at] = shares
         out = jnp.transpose(per_head(kvt[LW:, :], shares)).astype(BF)
         ats[k] = out.reshape(NV, CH, LW)
-        for j in order + (0,):
-            to = (plus(v, j, NV), plus(s, -k, NSP))
-            if k or j:
-                push(ats.at[k, to[0]], att.at[s, j], ("view", "space"), to, a_out[min(k, 1)], a_num[k])
-            else:
-                att[pl.ds(s, 1), 0:1] = ats[0:1, pl.ds(v, 1)]
+
+        def send(dz, dy):
+            place, *to = home(dz, dy)
+            to.append(plus(s, -k, NSP))
+            push(ats.at[k, place], att.at[s, v], ("tm", "view", "space"), to, a_out[min(k, 1)], a_num[k])
+
+        for dz, dy in homes[:-1]:
+            send(dz, dy)
+        if k:
+            send(0, 0)
+        else:
+
+            def keep():
+                att[pl.ds(s, 1), pl.ds(v, 1)] = ats[0:1, pl.ds(piece, 1)]
+
+            unless_alone(lambda: send(0, 0), keep)
 
     attend_space(2)
     g_a.b()
@@ -284,18 +329,16 @@
     g_b.c()
     g_a.d()
 
-    def slot_of(view):
-        return lax.rem(v - view + NV, NV)
-
     g_b.d()
-    landed(xb.at[1:NV], x2_num)
+    landed_all(xb, x2_num)
     for k in (2, 1, 3):
         landed(att.at[plus(s, k, NSP)], a_num[k])
-    landed(att.at[s, 1:NV], a_num[0])
+    landed_all(att.at[s], a_num[0])
     c2_num, c2_out = ticket(), sending(c2.at[1:NT_])
-    for m in tm_order:
-        push(xb.at[slot_of(paired(m)), 1], c2.at[m], "tm", paired(m), c2_out, c2_num)
-    c2[0] = xb[slot_of(t), 1]
+    for m in members:
+        to, its_frame = member(m)
+        push(xb.at[its_frame, 1], c2.at[m], ("tm", "view"), to, c2_out, c2_num)
+    c2[0] = xb[frame, 1]
     g_c.b()
     g_a.e()
     term = dot(att[0].reshape(TOK, LW), wos[0, :LW, :], NN)
@@ -341,9 +384,10 @@
     xt[...] = (rows_view.astype(F32) + term).astype(BF).reshape(NV, CH, D)
 
     x3_num, x3_out = ticket(), sending(x3.at[1:NT_])
-    for m in tm_order:
-        push(xt.at[slot_of(paired(m))], x3.at[m], "tm", paired(m), x3_out, x3_num)
-    x3[0] = xt[slot_of(t)]
+    for m in members:
+        to, its_frame = member(m)
+        push(xt.at[its_frame], x3.at[m], ("tm", "view"), to, x3_out, x3_num)
+    x3[0] = xt[frame]
     g_c.d()
     landed(c2.at[1:NT_], c2_num)
     upstream = c2[...].reshape(TOK, D)
@@ -362,10 +406,9 @@
     ut[...] = finish(upstream, rows_time, total).reshape(NT_, CH, D)
 
     u2_num, u2_out = ticket(), sending(ut.at[1:NT_])
-    here = slot_of(t)
-    for m in tm_order:
-        push(ut.at[m], u2.at[here], "tm", paired(m), u2_out, u2_num)
-    u2[pl.ds(here, 1)] = ut[0:1]
+    for m in members:
+        push(ut.at[m], u2.at[frame], ("tm", "view"), member(m)[0], u2_out, u2_num)
+    u2[pl.ds(frame, 1)] = ut[0:1]
     landed(u2.at[1:NT_], u2_num)
     upstream = u2[...].reshape(TOK, D)
     total = jnp.zeros((TOK, D), F32)
@@ -380,13 +423,22 @@
         part = jnp.transpose(out_grad[h * LW : (h + 1) * LW]).astype(BF)
         ogs[h] = part.reshape(NV, CH, LW)
     og_num = [ticket() for _ in range(NSP)]
-    og_out = sending(ogs.at[0, 1:NV]), sending(ogs.at[1:NSP])
+    og_out = sending(ogs.at[0], True), sending(ogs.at[1:NSP])
+    def send_out_grad(k, j):
+        to = (frame, plus(v, j, NV), plus(s, k, NSP))
+        numbers = og_out[min(k, 1)], og_num[k]
+        push(ogs.at[to[2], to[1]], og.at[k, piece], ("tm", "view", "space"), to, *numbers)
+
+    def keep_out_grad():
+        og[0:1, pl.ds(piece, 1)] = ogs[pl.ds(s, 1), pl.ds(v, 1)]
+
     for k in (2, 1, 3, 0):
-        for j in order + (0,):
-            to = (plus(v, -j, NV), plus(s, k, NSP))
-            if k or j:
-                push(ogs.at[to[1], j], og.at[k, v], ("view", "space"), to, og_out[min(k, 1)], og_num[k])
-    og[0:1, pl.ds(v, 1)] = ogs[pl.ds(s, 1), 0:1]
+        for j in order:
+            send_out_grad(k, j)
+        if k:
+            send_out_grad(k, 0)
+    unless_alone(lambda: send_out_grad(0, 0), keep_out_grad)
+
     def backward_space(k):
         at = slice(k * LH * TOK, (k + 1) * LH * TOK)
         out_grad = og[k].reshape(TOK, LW)
@@ -401,14 +453,25 @@
 
     head_at = lax.broadcasted_iota(jnp.int32, (TOK, LW), 1) // HD
     nmask = [(head_at == h).astype(F32).astype(BF) for h in range(LH)]
-    u3_num, u3_out = ticket(), sending(uv.at[1:NV])
+    u3_num, u3_out = ticket(), sending(uv, True)
+
+    def send_upstream(j):
+        to = (frame, plus(v, j, NV))
+        push(uv.at[to[1]], u3.at[piece], ("tm", "view"), to, u3_out, u3_num)
+
+    def keep_upstream():
+        u3[pl.ds(piece, 1)] = uv[pl.ds(v, 1)]
+
     for k in (0, 1, 3, 2):
-        landed(og.at[k] if k else og.at[0, 1:NV], og_num[k])
+        if k:
+            landed(og.at[k], og_num[k])
+        else:
+            landed_all(og.at[0], og_num[0])
         if k == 2:
             for j in order:
-                push(uv.at[j], u3.at[v], "view", plus(v, -j, NV), u3_out, u3_num)
+                send_upstream(j)
+            unless_alone(lambda: send_upstream(0), keep_upstream)
         backward_space(k)
-    u3[pl.ds(v, 1)] = uv[0:1]
 
     def partial_sums(k):
         at = pl.ds(pl.multiple_of(k * TOK, TOK), TOK)
@@ -433,11 +496,20 @@
     total += rs[0].astype(F32)
     landed(rs.at[1], late_num)
     total += rs[1].astype(F32)
-    landed(u3.at[1:NV], u3_num)
+    landed_all(u3, u3_num)
     out_ref[...] = finish(u3[...].reshape(TOK, D), xc[:, 0].reshape(TOK, D), total)
 
-    for ref, number in left:
+    def gone(ref, number):
         remote(ref, ref, "tm", sibling, number, 0).wait_send()
+
+    for ref, number, eight in left:
+        if eight:
+            unless_alone(
+                lambda ref=ref, number=number: gone(ref, number),
+                lambda ref=ref, number=number: gone(ref.at[1:], number),
+            )
+        else:
+            gone(ref, number)
 
 
 def on_device(latents, cotangent, wqs, wos, wqv, wov, wqt, wot):

time: 99.9 us -> 103 us (1.031)
  Pallas kernels: 98.1 us -> 101 us
    pallas_call x1, Pallas kernels: 98.1 us -> 101 us  [on_device(): pl.pallas_call(body, out_shape=jax.ShapeDtypeStruct((TOK, D), BF), in_spe...]
where the time goes in v5:
time: 103 us
  Pallas kernels  101 us (98%)
  local copies, waits for them, and re-layouts  1.62 us (2%)
    pallas_call x1, Pallas kernels, on_device(): pl.pallas_call(body, out_shape=jax.ShapeDtypeStruct((TOK, D), BF), in_spe...  101 us

profile of v5, /device:TPU:2, one launch (start us, length us, event | category | flops | bytes accessed | tf_op | source)
XLA Modules:
  0.0 102.6 jit_solution(10935973811835517147)
XLA Ops:
  0.0 100.9 %block_backward.1 = bf16[128,768]{1,0:T(8,128)(2,1)} custom-call(bf16[8,16,768]{2,1,0:T(8,128)(2,1)} %bitcast.12, bf16[8,16,768]{2,1,0:T(8,128)(2,1)} %bitcast.13, bf16[576,768]{1,0:T(8,128)(2,1)} %bitcast.7, bf16[1,192,768]{2,1,0:T(8,128)(2,1)} %bitcast.9, bf16[3,192,768]{2,1,0:T(8,128)(2,1)} %wqv_in.1, bf16[1,192,768]{2,1,0:T(8,128)(2,1)} %bitcast.10, ...), custom_call_target="tpu_custom_call" | custom-call | tf_op jit(solution)/shard_map/block_backward/pallas_call | solution.py:523
  100.9 1.6 %copy.10 = bf16[1,1,128,768]{3,2,1,0:T(8,128)(2,1)} copy(bf16[1,1,128,768]{3,2,1,0:T(8,128)(2,1)} %bitcast.8) | data formatting | bytes 393216

commit v6 on v4

--- a/solution.py
+++ b/solution.py
@@ -265,6 +265,8 @@
         pts[:, at] = shares
         out = jnp.transpose(per_head(kvt[LW:, :], shares)).astype(BF)
         ats[k] = out.reshape(NV, CH, LW)
+
+    def send_attended(k):
         for j in order + (0,):
             to = (plus(v, j, NV), plus(s, -k, NSP))
             if k or j:
@@ -273,16 +275,20 @@
                 att[pl.ds(s, 1), 0:1] = ats[0:1, pl.ds(v, 1)]
 
     attend_space(2)
+    attend_space(1)
+    send_attended(2)
+    send_attended(1)
     g_a.b()
     g_b.a()
-    attend_space(1)
     attend_space(3)
+    attend_space(0)
+    send_attended(3)
+    send_attended(0)
     g_a.c()
     g_b.b()
     g_c.a()
-    attend_space(0)
+    g_a.d()
     g_b.c()
-    g_a.d()
 
     def slot_of(view):
         return lax.rem(v - view + NV, NV)
@@ -334,8 +340,7 @@
         queries, key_t, value_t, shares = attend_small(wqv, g)
         qts_v[g], kt_v[g], vt_v[g], pt_v[g] = queries, key_t, value_t, shares
         outs.append(per_head(value_t, shares).astype(BF))
-        if g == 0:
-            g_c.c()
+    g_c.c()
     g_b.e()
     term = dot(jnp.concatenate(outs, axis=0), wov[0], TN)
     xt[...] = (rows_view.astype(F32) + term).astype(BF).reshape(NV, CH, D)
@@ -402,12 +407,16 @@
     head_at = lax.broadcasted_iota(jnp.int32, (TOK, LW), 1) // HD
     nmask = [(head_at == h).astype(F32).astype(BF) for h in range(LH)]
     u3_num, u3_out = ticket(), sending(uv.at[1:NV])
-    for k in (0, 1, 3, 2):
-        landed(og.at[k] if k else og.at[0, 1:NV], og_num[k])
-        if k == 2:
-            for j in order:
-                push(uv.at[j], u3.at[v], "view", plus(v, -j, NV), u3_out, u3_num)
-        backward_space(k)
+    landed(og.at[0, 1:NV], og_num[0])
+    landed(og.at[1], og_num[1])
+    backward_space(0)
+    backward_space(1)
+    landed(og.at[3], og_num[3])
+    landed(og.at[2], og_num[2])
+    for j in order:
+        push(uv.at[j], u3.at[v], "view", plus(v, -j, NV), u3_out, u3_num)
+    backward_space(3)
+    backward_space(2)
     u3[pl.ds(v, 1)] = uv[0:1]
 
     def partial_sums(k):
@@ -425,10 +434,10 @@
     rsend[1] = partial_sums(1 + 2 * core).astype(BF)
     push(rsend.at[1], rs.at[0], "space", s_prev, rs_out, near_num)
     late = partial_sums(3 - 2 * core)
+    total = partial_sums(0)
     landed(rf, rf_num)
     rsend[2] = (late + rf[...].astype(F32)).astype(BF)
     push(rsend.at[2], rs.at[1], "space", s_next, rs_out, late_num)
-    total = partial_sums(0)
     landed(rs.at[0], near_num)
     total += rs[0].astype(F32)
     landed(rs.at[1], late_num)

time: 99.9 us -> 97 us (0.971)
  Pallas kernels: 98.1 us -> 94.4 us
    pallas_call x1, Pallas kernels: 98.1 us -> 94.4 us  [on_device(): pl.pallas_call(body, out_shape=jax.ShapeDtypeStruct((TOK, D), BF), in_spe...]
where the time goes in v6:
time: 97 us; the launch traced here: 96.1 us
  Pallas kernels  94.4 us (97%)
  local copies, waits for them, and re-layouts  1.62 us (2%)
    pallas_call x1, Pallas kernels, on_device(): pl.pallas_call(body, out_shape=jax.ShapeDtypeStruct((TOK, D), BF), in_spe...  94.4 us

profile of v6, /device:TPU:2, one launch (start us, length us, event | category | flops | bytes accessed | tf_op | source)
XLA Modules:
  0.0 96.1 jit_solution(10181125397218870838)
XLA Ops:
  0.0 94.4 %block_backward.1 = bf16[128,768]{1,0:T(8,128)(2,1)} custom-call(bf16[8,16,768]{2,1,0:T(8,128)(2,1)} %bitcast.12, bf16[8,16,768]{2,1,0:T(8,128)(2,1)} %bitcast.13, bf16[576,768]{1,0:T(8,128)(2,1)} %bitcast.7, bf16[1,192,768]{2,1,0:T(8,128)(2,1)} %bitcast.9, bf16[3,192,768]{2,1,0:T(8,128)(2,1)} %wqv_in.1, bf16[1,192,768]{2,1,0:T(8,128)(2,1)} %bitcast.10, ...), custom_call_target="tpu_custom_call" | custom-call | tf_op jit(solution)/shard_map/block_backward/pallas_call | solution.py:460
  94.4 1.6 %copy.10 = bf16[1,1,128,768]{3,2,1,0:T(8,128)(2,1)} copy(bf16[1,1,128,768]{3,2,1,0:T(8,128)(2,1)} %bitcast.8) | data formatting | bytes 393216

commit v7 on v6

--- a/solution.py
+++ b/solution.py
@@ -295,6 +295,7 @@
 
     g_b.d()
     landed(xb.at[1:NV], x2_num)
+    g_c.b()
     for k in (2, 1, 3):
         landed(att.at[plus(s, k, NSP)], a_num[k])
     landed(att.at[s, 1:NV], a_num[0])
@@ -302,7 +303,6 @@
     for m in tm_order:
         push(xb.at[slot_of(paired(m)), 1], c2.at[m], "tm", paired(m), c2_out, c2_num)
     c2[0] = xb[slot_of(t), 1]
-    g_c.b()
     g_a.e()
     term = dot(att[0].reshape(TOK, LW), wos[0, :LW, :], NN)
     for h in range(1, NSP):
@@ -335,12 +335,13 @@
         total += dot(key_grad, w[1, lanes, :], NN)
         return total + dot(value_grad, w[2, lanes, :], NN)
 
+    g_c.c()
     outs = []
     for g in range(GROUPS):
         queries, key_t, value_t, shares = attend_small(wqv, g)
         qts_v[g], kt_v[g], vt_v[g], pt_v[g] = queries, key_t, value_t, shares
         outs.append(per_head(value_t, shares).astype(BF))
-    g_c.c()
+    g_c.d()
     g_b.e()
     term = dot(jnp.concatenate(outs, axis=0), wov[0], TN)
     xt[...] = (rows_view.astype(F32) + term).astype(BF).reshape(NV, CH, D)
@@ -349,7 +350,6 @@
     for m in tm_order:
         push(xt.at[slot_of(paired(m))], x3.at[m], "tm", paired(m), x3_out, x3_num)
     x3[0] = xt[slot_of(t)]
-    g_c.d()
     landed(c2.at[1:NT_], c2_num)
     upstream = c2[...].reshape(TOK, D)
     out_grads = dot(wot[0], upstream, NT).astype(BF)

time: 97 us -> 102 us (1.052)
  Pallas kernels: 94.4 us -> 99.2 us
    pallas_call x1, Pallas kernels: 94.4 us -> 99.2 us  [on_device(): pl.pallas_call(body, out_shape=jax.ShapeDtypeStruct((TOK, D), BF), in_spe...]
where the time goes in v7:
time: 102 us; the launch traced here: 101 us
  Pallas kernels  99.2 us (97%)
  local copies, waits for them, and re-layouts  1.62 us (2%)
    pallas_call x1, Pallas kernels, on_device(): pl.pallas_call(body, out_shape=jax.ShapeDtypeStruct((TOK, D), BF), in_spe...  99.2 us

profile of v7, /device:TPU:2, one launch (start us, length us, event | category | flops | bytes accessed | tf_op | source)
XLA Modules:
  0.0 100.8 jit_solution(13572834695694425933)
XLA Ops:
  0.0 99.2 %block_backward.1 = bf16[128,768]{1,0:T(8,128)(2,1)} custom-call(bf16[8,16,768]{2,1,0:T(8,128)(2,1)} %bitcast.12, bf16[8,16,768]{2,1,0:T(8,128)(2,1)} %bitcast.13, bf16[576,768]{1,0:T(8,128)(2,1)} %bitcast.7, bf16[1,192,768]{2,1,0:T(8,128)(2,1)} %bitcast.9, bf16[3,192,768]{2,1,0:T(8,128)(2,1)} %wqv_in.1, bf16[1,192,768]{2,1,0:T(8,128)(2,1)} %bitcast.10, ...), custom_call_target="tpu_custom_call" | custom-call | tf_op jit(solution)/shard_map/block_backward/pallas_call | solution.py:460
  99.2 1.6 %copy.10 = bf16[1,1,128,768]{3,2,1,0:T(8,128)(2,1)} copy(bf16[1,1,128,768]{3,2,1,0:T(8,128)(2,1)} %bitcast.8) | data formatting | bytes 393216

commit v8 on v6

--- a/solution.py
+++ b/solution.py
@@ -25,7 +25,7 @@
 GW = GH * HD
 GROUPS = D // GW
 SCALE = HD**-0.5
-NSEM = 64
+NSEM = 128
 
 
 def dot(a, b, dims):
@@ -173,8 +173,8 @@
         def e(self):
             landed(self.bytes_of(288), self.sib)
 
-    g_a, g_b, g_c = Gather(0, 4), Gather(4, 6), Gather(6, 9)
-    wos, wqv, wov = whole.at[0:1], whole.at[1:4], whole.at[4:5]
+    g_a1, g_a2, g_b, g_c = Gather(0, 2), Gather(2, 4), Gather(4, 6), Gather(6, 9)
+    wqv, wos, wov = whole.at[0:3], whole.at[3:4], whole.at[4:5]
     wot, wqt = whole.at[5:6], whole.at[6:9]
     own = pl.ds(pl.multiple_of(s * LW, 16), LW)
 
@@ -228,6 +228,7 @@
             push(nb.at[0, part], nb.at[k, part], "space", plus(s, k, NSP), n_out[0], n_near[h])
     for copy in loads[1:]:
         copy.wait()
+    g_a1.a()
     order = (4, 3, 5, 2, 6, 1, 7)
     x2_num, x2_out = ticket(), sending(xb.at[1:NV])
     for j in order:
@@ -249,9 +250,10 @@
     for h, part in enumerate(halves):
         landed(nb.at[0], n_near[h])
         push(nb.at[1 + 2 * core, part], nb.at[2, part], "space", s_next, n_out[1], n_far[h])
-    g_a.a()
+    g_a2.a()
     project_space(1)
     project_space(3)
+    g_a1.b()
     for h, part in enumerate(halves):
         landed(nb.at[2, part], n_far[h])
     project_space(2)
@@ -278,22 +280,23 @@
     attend_space(1)
     send_attended(2)
     send_attended(1)
-    g_a.b()
+    g_a2.b()
+    g_a1.c()
     g_b.a()
     attend_space(3)
     attend_space(0)
     send_attended(3)
     send_attended(0)
-    g_a.c()
+    g_a2.c()
+    g_a1.d()
     g_b.b()
     g_c.a()
-    g_a.d()
+    g_a2.d()
     g_b.c()
 
     def slot_of(view):
         return lax.rem(v - view + NV, NV)
 
-    g_b.d()
     landed(xb.at[1:NV], x2_num)
     for k in (2, 1, 3):
         landed(att.at[plus(s, k, NSP)], a_num[k])
@@ -302,8 +305,10 @@
     for m in tm_order:
         push(xb.at[slot_of(paired(m)), 1], c2.at[m], "tm", paired(m), c2_out, c2_num)
     c2[0] = xb[slot_of(t), 1]
+    g_b.d()
     g_c.b()
-    g_a.e()
+    g_a1.e()
+    g_a2.e()
     term = dot(att[0].reshape(TOK, LW), wos[0, :LW, :], NN)
     for h in range(1, NSP):
         term += dot(att[h].reshape(TOK, LW), wos[0, h * LW : (h + 1) * LW, :], NN)

time: 97 us -> 97.2 us (level)
  Pallas kernels: 94.4 us -> 95.5 us
    pallas_call x1, Pallas kernels: 94.4 us -> 95.5 us  [on_device(): pl.pallas_call(body, out_shape=jax.ShapeDtypeStruct((TOK, D), BF), in_spe...]
where the time goes in v8:
time: 97.2 us; the launch traced here: 97.1 us
  Pallas kernels  95.5 us (98%)
  local copies, waits for them, and re-layouts  1.62 us (2%)
    pallas_call x1, Pallas kernels, on_device(): pl.pallas_call(body, out_shape=jax.ShapeDtypeStruct((TOK, D), BF), in_spe...  95.5 us

profile of v8, /device:TPU:2, one launch (start us, length us, event | category | flops | bytes accessed | tf_op | source)
XLA Modules:
  0.0 97.1 jit_solution(15271269846745822671)
XLA Ops:
  0.0 95.5 %block_backward.1 = bf16[128,768]{1,0:T(8,128)(2,1)} custom-call(bf16[8,16,768]{2,1,0:T(8,128)(2,1)} %bitcast.12, bf16[8,16,768]{2,1,0:T(8,128)(2,1)} %bitcast.13, bf16[576,768]{1,0:T(8,128)(2,1)} %bitcast.7, bf16[1,192,768]{2,1,0:T(8,128)(2,1)} %bitcast.9, bf16[3,192,768]{2,1,0:T(8,128)(2,1)} %wqv_in.1, bf16[1,192,768]{2,1,0:T(8,128)(2,1)} %bitcast.10, ...), custom_call_target="tpu_custom_call" | custom-call | tf_op jit(solution)/shard_map/block_backward/pallas_call | solution.py:465
  95.5 1.6 %copy.10 = bf16[1,1,128,768]{3,2,1,0:T(8,128)(2,1)} copy(bf16[1,1,128,768]{3,2,1,0:T(8,128)(2,1)} %bitcast.8) | data formatting | bytes 393216

commit v9 on v6

--- a/solution.py
+++ b/solution.py
@@ -37,8 +37,7 @@
     return values * factor, factor
 
 
-def finish(upstream, earlier, normed_grad):
-    normed, factor = rms(earlier.astype(F32))
+def finish(upstream, normed, factor, normed_grad):
     inner = jnp.mean(normed_grad * normed, axis=-1, keepdims=True)
     return (upstream.astype(F32) + factor * (normed_grad - normed * inner)).astype(BF)
 
@@ -75,7 +74,7 @@
     xc, wqs_ref,
     nb, k_nat, v_nat, qts, kvt, pts, gts, ogts, dqt, ats, att,
     xb, x2, xt, x3, c2, ut, u2, uv, u3, ogs, og, rsend, rs, rf,
-    bias, kt_v, vt_v, qts_v, pt_v,
+    bias, kt_v, vt_v, v_v, qts_v, pt_v,
     whole,
     send_sem, recv_sem, local_sem,
 ):
@@ -321,19 +320,19 @@
         shares = softmax0(dot(key_t, queries, TN) + bias[...]).astype(BF)
         return queries, key_t, value_t, shares
 
-    def backward_small(w, g, queries, key_t, value_t, shares, out_grad):
-        lanes = slice(g * GW, (g + 1) * GW)
-        grads = stacked(out_grad, gmask)
-        share_grad = dot(value_t, grads, TN)
+    def backward_small(queries, key_t, value, shares, grads):
+        share_grad = dot(value, grads, NN)
         wide = shares.astype(F32)
         row_dot = jnp.sum(wide * share_grad, axis=0, keepdims=True)
         score_grad = (wide * (share_grad - row_dot)).astype(BF)
         query_grad = (per_head(key_t, score_grad) * SCALE).astype(BF)
         key_grad = dot(score_grad, queries, NT).astype(BF)
         value_grad = dot(shares, grads, NT).astype(BF)
-        total = dot(query_grad, w[0, lanes, :], TN)
-        total += dot(key_grad, w[1, lanes, :], NN)
-        return total + dot(value_grad, w[2, lanes, :], NN)
+        return jnp.transpose(query_grad), key_grad, value_grad
+
+    def normed_grad_of(parts, w):
+        columns = [part[at] for at in range(3) for part in parts]
+        return dot(jnp.concatenate(columns, axis=1), w[...].reshape(3 * D, D), NN)
 
     outs = []
     for g in range(GROUPS):
@@ -353,31 +352,36 @@
     landed(c2.at[1:NT_], c2_num)
     upstream = c2[...].reshape(TOK, D)
     out_grads = dot(wot[0], upstream, NT).astype(BF)
+    grads_t = [stacked(out_grads[g * GW : (g + 1) * GW], gmask) for g in range(GROUPS)]
+    for g in range(GROUPS):
+        v_v[g] = jnp.transpose(vt_v[g])
     landed(x3.at[1:NT_], x3_num)
     g_c.e()
     rows_time = x3[...].reshape(TOK, D)
-    normed, _ = rms(rows_time.astype(F32))
+    normed, factor = rms(rows_time.astype(F32))
     tokens = normed.astype(BF)
 
-    total = jnp.zeros((TOK, D), F32)
+    parts = []
     for g in range(GROUPS):
         queries, key_t, value_t, shares = attend_small(wqt, g)
-        out_grad = out_grads[g * GW : (g + 1) * GW]
-        total += backward_small(wqt, g, queries, key_t, value_t, shares, out_grad)
-    ut[...] = finish(upstream, rows_time, total).reshape(NT_, CH, D)
+        parts.append(backward_small(queries, key_t, jnp.transpose(value_t), shares, grads_t[g]))
+    total = normed_grad_of(parts, wqt)
+    ut[...] = finish(upstream, normed, factor, total).reshape(NT_, CH, D)
 
     u2_num, u2_out = ticket(), sending(ut.at[1:NT_])
     here = slot_of(t)
     for m in tm_order:
         push(ut.at[m], u2.at[here], "tm", paired(m), u2_out, u2_num)
     u2[pl.ds(here, 1)] = ut[0:1]
+    normed, factor = rms(x2[...].reshape(TOK, D).astype(F32))
     landed(u2.at[1:NT_], u2_num)
     upstream = u2[...].reshape(TOK, D)
-    total = jnp.zeros((TOK, D), F32)
+    parts = []
     for g in range(GROUPS):
         out_grad = dot(wov[0, g * GW : (g + 1) * GW, :], upstream, NT).astype(BF)
-        total += backward_small(wqv, g, qts_v[g], kt_v[g], vt_v[g], pt_v[g], out_grad)
-    upstream = finish(upstream, x2[...].reshape(TOK, D), total)
+        saved = qts_v[g], kt_v[g], v_v[g], pt_v[g]
+        parts.append(backward_small(*saved, stacked(out_grad, gmask)))
+    upstream = finish(upstream, normed, factor, normed_grad_of(parts, wqv))
     uv[...] = upstream.reshape(NV, CH, D)
 
     out_grad = dot(wos[0], upstream, NT)
@@ -438,12 +442,13 @@
     landed(rf, rf_num)
     rsend[2] = (late + rf[...].astype(F32)).astype(BF)
     push(rsend.at[2], rs.at[1], "space", s_next, rs_out, late_num)
+    normed, factor = rms(xc[:, 0].reshape(TOK, D).astype(F32))
     landed(rs.at[0], near_num)
     total += rs[0].astype(F32)
     landed(rs.at[1], late_num)
     total += rs[1].astype(F32)
     landed(u3.at[1:NV], u3_num)
-    out_ref[...] = finish(u3[...].reshape(TOK, D), xc[:, 0].reshape(TOK, D), total)
+    out_ref[...] = finish(u3[...].reshape(TOK, D), normed, factor, total)
 
     for ref, number in left:
         remote(ref, ref, "tm", sibling, number, 0).wait_send()
@@ -488,6 +493,7 @@
             buf(TOK, GH * TOK, dtype=F32),
             buf(GROUPS, GW, TOK),
             buf(GROUPS, GW, TOK),
+            buf(GROUPS, TOK, GW),
             buf(GROUPS, GW, GH * TOK),
             buf(GROUPS, TOK, GH * TOK),
             buf(9, D, D),

time: 97 us -> 96.1 us (level)
  no operation moved by 1% of the time
where the time goes in v9:
time: 96.1 us; the launch traced here: 95.7 us
  Pallas kernels  94.1 us (98%)
  local copies, waits for them, and re-layouts  1.62 us (2%)
    pallas_call x1, Pallas kernels, on_device(): pl.pallas_call(body, out_shape=jax.ShapeDtypeStruct((TOK, D), BF), in_spe...  94.1 us

profile of v9, /device:TPU:2, one launch (start us, length us, event | category | flops | bytes accessed | tf_op | source)
XLA Modules:
  0.0 95.7 jit_solution(13161902549787830124)
XLA Ops:
  0.0 94.1 %block_backward.1 = bf16[128,768]{1,0:T(8,128)(2,1)} custom-call(bf16[8,16,768]{2,1,0:T(8,128)(2,1)} %bitcast.12, bf16[8,16,768]{2,1,0:T(8,128)(2,1)} %bitcast.13, bf16[576,768]{1,0:T(8,128)(2,1)} %bitcast.7, bf16[1,192,768]{2,1,0:T(8,128)(2,1)} %bitcast.9, bf16[3,192,768]{2,1,0:T(8,128)(2,1)} %wqv_in.1, bf16[1,192,768]{2,1,0:T(8,128)(2,1)} %bitcast.10, ...), custom_call_target="tpu_custom_call" | custom-call | tf_op jit(solution)/shard_map/block_backward/pallas_call | solution.py:465
  94.1 1.6 %copy.10 = bf16[1,1,128,768]{3,2,1,0:T(8,128)(2,1)} copy(bf16[1,1,128,768]{3,2,1,0:T(8,128)(2,1)} %bitcast.8) | data formatting | bytes 393216

commit v10 on v9

--- a/solution.py
+++ b/solution.py
@@ -26,6 +26,7 @@
 GROUPS = D // GW
 SCALE = HD**-0.5
 NSEM = 64
+VMEM = 859 * 65536
 
 
 def dot(a, b, dims):
@@ -123,6 +124,9 @@
     def landed(ref, arrival):
         remote(ref, ref, "tm", sibling, 0, arrival).wait_recv()
 
+    def gone(ref, number):
+        remote(ref, ref, "tm", sibling, number, 0).wait_send()
+
     def sending(ref):
         left.append((ref, ticket()))
         return left[-1][1]
@@ -374,6 +378,9 @@
         push(ut.at[m], u2.at[here], "tm", paired(m), u2_out, u2_num)
     u2[pl.ds(here, 1)] = ut[0:1]
     normed, factor = rms(x2[...].reshape(TOK, D).astype(F32))
+    for ref, number in left[:-1]:
+        gone(ref, number)
+    del left[:-1]
     landed(u2.at[1:NT_], u2_num)
     upstream = u2[...].reshape(TOK, D)
     parts = []
@@ -431,27 +438,31 @@
         part += dot(key_grad, wqs_ref[LW : 2 * LW, :], NN)
         return part + dot(value_grad, wqs_ref[2 * LW :, :], NN)
 
-    rf_num, near_num, late_num = ticket(), ticket(), ticket()
+    rf_num, late_num = [ticket() for _ in halves], [ticket() for _ in halves]
+    near_num = ticket()
     rs_out = sending(rsend)
     rsend[0] = partial_sums(2).astype(BF)
-    push(rsend.at[0], rf, "space", s_next, rs_out, rf_num)
+    for h, part in enumerate(halves):
+        push(rsend.at[0, part], rf.at[part], "space", s_next, rs_out, rf_num[h])
     rsend[1] = partial_sums(1 + 2 * core).astype(BF)
     push(rsend.at[1], rs.at[0], "space", s_prev, rs_out, near_num)
     late = partial_sums(3 - 2 * core)
     total = partial_sums(0)
-    landed(rf, rf_num)
-    rsend[2] = (late + rf[...].astype(F32)).astype(BF)
-    push(rsend.at[2], rs.at[1], "space", s_next, rs_out, late_num)
     normed, factor = rms(xc[:, 0].reshape(TOK, D).astype(F32))
+    for h, part in enumerate(halves):
+        landed(rf.at[part], rf_num[h])
+        rsend[2, part] = (late[part] + rf[part].astype(F32)).astype(BF)
+        push(rsend.at[2, part], rs.at[1, part], "space", s_next, rs_out, late_num[h])
     landed(rs.at[0], near_num)
     total += rs[0].astype(F32)
-    landed(rs.at[1], late_num)
+    for h, part in enumerate(halves):
+        landed(rs.at[1, part], late_num[h])
     total += rs[1].astype(F32)
     landed(u3.at[1:NV], u3_num)
     out_ref[...] = finish(u3[...].reshape(TOK, D), normed, factor, total)
 
     for ref, number in left:
-        remote(ref, ref, "tm", sibling, number, 0).wait_send()
+        gone(ref, number)
 
 
 def on_device(latents, cotangent, wqs, wos, wqv, wov, wqt, wot):
@@ -502,7 +513,7 @@
             pltpu.SemaphoreType.DMA((8,)),
         ],
         compiler_params=pltpu.CompilerParams(
-            collective_id=0, has_side_effects=True, vmem_limit_bytes=60 * 1024 * 1024
+            collective_id=0, has_side_effects=True, vmem_limit_bytes=VMEM
         ),
         name="block_backward",
     )(

time: 96.1 us -> 93.3 us (0.971)
  Pallas kernels: 94.1 us -> 92.3 us
    pallas_call x1, Pallas kernels: 94.1 us -> 92.3 us  [on_device(): pl.pallas_call(body, out_shape=jax.ShapeDtypeStruct((TOK, D), BF), in_spe...]
where the time goes in v10:
time: 93.3 us; the launch traced here: 93 us
  Pallas kernels  92.3 us (99%)
    pallas_call x1, Pallas kernels, on_device(): pl.pallas_call(body, out_shape=jax.ShapeDtypeStruct((TOK, D), BF), in_spe...  92.3 us

profile of v10, /device:TPU:2, one launch (start us, length us, event | category | flops | bytes accessed | tf_op | source)
XLA Modules:
  0.0 93.0 jit_solution(787590304613383551)
XLA Ops:
  0.0 92.3 %block_backward.1 = bf16[128,768]{1,0:T(8,128)(2,1)S(1)} custom-call(bf16[8,16,768]{2,1,0:T(8,128)(2,1)} %bitcast.12, bf16[8,16,768]{2,1,0:T(8,128)(2,1)} %bitcast.13, bf16[576,768]{1,0:T(8,128)(2,1)} %bitcast.8, bf16[1,192,768]{2,1,0:T(8,128)(2,1)} %bitcast.9, bf16[3,192,768]{2,1,0:T(8,128)(2,1)} %wqv_in.1, bf16[1,192,768]{2,1,0:T(8,128)(2,1)} %bitcast.10, ...), custom_call_target="tpu_custom_call" | custom-call | tf_op jit(solution)/shard_map/block_backward/pallas_call | solution.py:476
  92.3 0.7 copy.10

commit v11 on v10

--- a/solution.py
+++ b/solution.py
@@ -343,7 +343,8 @@
         queries, key_t, value_t, shares = attend_small(wqv, g)
         qts_v[g], kt_v[g], vt_v[g], pt_v[g] = queries, key_t, value_t, shares
         outs.append(per_head(value_t, shares).astype(BF))
-    g_c.c()
+        if g == 1:
+            g_c.c()
     g_b.e()
     term = dot(jnp.concatenate(outs, axis=0), wov[0], TN)
     xt[...] = (rows_view.astype(F32) + term).astype(BF).reshape(NV, CH, D)
@@ -352,13 +353,13 @@
     for m in tm_order:
         push(xt.at[slot_of(paired(m))], x3.at[m], "tm", paired(m), x3_out, x3_num)
     x3[0] = xt[slot_of(t)]
-    g_c.d()
     landed(c2.at[1:NT_], c2_num)
     upstream = c2[...].reshape(TOK, D)
     out_grads = dot(wot[0], upstream, NT).astype(BF)
     grads_t = [stacked(out_grads[g * GW : (g + 1) * GW], gmask) for g in range(GROUPS)]
     for g in range(GROUPS):
         v_v[g] = jnp.transpose(vt_v[g])
+    g_c.d()
     landed(x3.at[1:NT_], x3_num)
     g_c.e()
     rows_time = x3[...].reshape(TOK, D)

time: 93.3 us -> 96.6 us (1.035)
  Pallas kernels: 92.3 us -> 95.8 us
    pallas_call x1, Pallas kernels: 92.3 us -> 95.8 us  [on_device(): pl.pallas_call(body, out_shape=jax.ShapeDtypeStruct((TOK, D), BF), in_spe...]
where the time goes in v11:
time: 96.6 us; the launch traced here: 96.5 us
  Pallas kernels  95.8 us (99%)
    pallas_call x1, Pallas kernels, on_device(): pl.pallas_call(body, out_shape=jax.ShapeDtypeStruct((TOK, D), BF), in_spe...  95.8 us

profile of v11, /device:TPU:2, one launch (start us, length us, event | category | flops | bytes accessed | tf_op | source)
XLA Modules:
  0.0 96.5 jit_solution(6261645681523089500)
XLA Ops:
  0.0 95.8 %block_backward.1 = bf16[128,768]{1,0:T(8,128)(2,1)S(1)} custom-call(bf16[8,16,768]{2,1,0:T(8,128)(2,1)} %bitcast.12, bf16[8,16,768]{2,1,0:T(8,128)(2,1)} %bitcast.13, bf16[576,768]{1,0:T(8,128)(2,1)} %bitcast.8, bf16[1,192,768]{2,1,0:T(8,128)(2,1)} %bitcast.9, bf16[3,192,768]{2,1,0:T(8,128)(2,1)} %wqv_in.1, bf16[1,192,768]{2,1,0:T(8,128)(2,1)} %bitcast.10, ...), custom_call_target="tpu_custom_call" | custom-call | tf_op jit(solution)/shard_map/block_backward/pallas_call | solution.py:477
  95.8 0.7 copy.10

commit v12 on v11

--- a/solution.py
+++ b/solution.py
@@ -343,8 +343,6 @@
         queries, key_t, value_t, shares = attend_small(wqv, g)
         qts_v[g], kt_v[g], vt_v[g], pt_v[g] = queries, key_t, value_t, shares
         outs.append(per_head(value_t, shares).astype(BF))
-        if g == 1:
-            g_c.c()
     g_b.e()
     term = dot(jnp.concatenate(outs, axis=0), wov[0], TN)
     xt[...] = (rows_view.astype(F32) + term).astype(BF).reshape(NV, CH, D)
@@ -353,6 +351,7 @@
     for m in tm_order:
         push(xt.at[slot_of(paired(m))], x3.at[m], "tm", paired(m), x3_out, x3_num)
     x3[0] = xt[slot_of(t)]
+    g_c.c()
     landed(c2.at[1:NT_], c2_num)
     upstream = c2[...].reshape(TOK, D)
     out_grads = dot(wot[0], upstream, NT).astype(BF)

time: 96.6 us -> 94.7 us (0.980)
  the two profiles are of different devices: /device:TPU:2 before, /device:TPU:32 now
where the time goes in v12:
time: 94.7 us; the launch traced here: 94.6 us
  Pallas kernels  93.9 us (99%)
    pallas_call x1, Pallas kernels, on_device(): pl.pallas_call(body, out_shape=jax.ShapeDtypeStruct((TOK, D), BF), in_spe...  93.9 us

profile of v12, /device:TPU:32, one launch (start us, length us, event | category | flops | bytes accessed | tf_op | source)
XLA Modules:
  0.0 94.6 jit_solution(353601120730105480)
XLA Ops:
  0.0 93.9 %block_backward.1 = bf16[128,768]{1,0:T(8,128)(2,1)S(1)} custom-call(bf16[8,16,768]{2,1,0:T(8,128)(2,1)} %bitcast.12, bf16[8,16,768]{2,1,0:T(8,128)(2,1)} %bitcast.13, bf16[576,768]{1,0:T(8,128)(2,1)} %bitcast.8, bf16[1,192,768]{2,1,0:T(8,128)(2,1)} %bitcast.9, bf16[3,192,768]{2,1,0:T(8,128)(2,1)} %wqv_in.1, bf16[1,192,768]{2,1,0:T(8,128)(2,1)} %bitcast.10, ...), custom_call_target="tpu_custom_call" | custom-call | tf_op jit(solution)/shard_map/block_backward/pallas_call | solution.py:476
  93.9 0.7 copy.10

commit v13 on v12

--- a/solution.py
+++ b/solution.py
@@ -343,6 +343,7 @@
         queries, key_t, value_t, shares = attend_small(wqv, g)
         qts_v[g], kt_v[g], vt_v[g], pt_v[g] = queries, key_t, value_t, shares
         outs.append(per_head(value_t, shares).astype(BF))
+    g_c.c()
     g_b.e()
     term = dot(jnp.concatenate(outs, axis=0), wov[0], TN)
     xt[...] = (rows_view.astype(F32) + term).astype(BF).reshape(NV, CH, D)
@@ -351,7 +352,6 @@
     for m in tm_order:
         push(xt.at[slot_of(paired(m))], x3.at[m], "tm", paired(m), x3_out, x3_num)
     x3[0] = xt[slot_of(t)]
-    g_c.c()
     landed(c2.at[1:NT_], c2_num)
     upstream = c2[...].reshape(TOK, D)
     out_grads = dot(wot[0], upstream, NT).astype(BF)

time: 94.7 us -> 93.3 us (0.985)
  the two profiles are of different devices: /device:TPU:32 before, /device:TPU:2 now
where the time goes in v13:
time: 93.3 us; the launch traced here: 93.2 us
  Pallas kernels  92.5 us (99%)
    pallas_call x1, Pallas kernels, on_device(): pl.pallas_call(body, out_shape=jax.ShapeDtypeStruct((TOK, D), BF), in_spe...  92.5 us

profile of v13, /device:TPU:2, one launch (start us, length us, event | category | flops | bytes accessed | tf_op | source)
XLA Modules:
  0.0 93.2 jit_solution(7250269648288537955)
XLA Ops:
  0.0 92.5 %block_backward.1 = bf16[128,768]{1,0:T(8,128)(2,1)S(1)} custom-call(bf16[8,16,768]{2,1,0:T(8,128)(2,1)} %bitcast.12, bf16[8,16,768]{2,1,0:T(8,128)(2,1)} %bitcast.13, bf16[576,768]{1,0:T(8,128)(2,1)} %bitcast.8, bf16[1,192,768]{2,1,0:T(8,128)(2,1)} %bitcast.9, bf16[3,192,768]{2,1,0:T(8,128)(2,1)} %wqv_in.1, bf16[1,192,768]{2,1,0:T(8,128)(2,1)} %bitcast.10, ...), custom_call_target="tpu_custom_call" | custom-call | tf_op jit(solution)/shard_map/block_backward/pallas_call | solution.py:476
  92.5 0.7 copy.10

commit v14 on v10

--- a/solution.py
+++ b/solution.py
@@ -419,15 +419,12 @@
     nmask = [(head_at == h).astype(F32).astype(BF) for h in range(LH)]
     u3_num, u3_out = ticket(), sending(uv.at[1:NV])
     landed(og.at[0, 1:NV], og_num[0])
-    landed(og.at[1], og_num[1])
-    backward_space(0)
-    backward_space(1)
-    landed(og.at[3], og_num[3])
-    landed(og.at[2], og_num[2])
+    for k in (1, 3, 2):
+        landed(og.at[k], og_num[k])
     for j in order:
         push(uv.at[j], u3.at[v], "view", plus(v, -j, NV), u3_out, u3_num)
-    backward_space(3)
-    backward_space(2)
+    for k in range(NSP):
+        backward_space(k)
     u3[pl.ds(v, 1)] = uv[0:1]
 
     def partial_sums(k):

time: 93.3 us -> 93.6 us (level)
  no operation moved by 1% of the time
where the time goes in v14:
time: 93.6 us
  Pallas kernels  92.9 us (99%)
    pallas_call x1, Pallas kernels, on_device(): pl.pallas_call(body, out_shape=jax.ShapeDtypeStruct((TOK, D), BF), in_spe...  92.9 us

profile of v14, /device:TPU:2, one launch (start us, length us, event | category | flops | bytes accessed | tf_op | source)
XLA Modules:
  0.0 93.6 jit_solution(15492782476456592592)
XLA Ops:
  0.0 92.9 %block_backward.1 = bf16[128,768]{1,0:T(8,128)(2,1)S(1)} custom-call(bf16[8,16,768]{2,1,0:T(8,128)(2,1)} %bitcast.12, bf16[8,16,768]{2,1,0:T(8,128)(2,1)} %bitcast.13, bf16[576,768]{1,0:T(8,128)(2,1)} %bitcast.8, bf16[1,192,768]{2,1,0:T(8,128)(2,1)} %bitcast.9, bf16[3,192,768]{2,1,0:T(8,128)(2,1)} %wqv_in.1, bf16[1,192,768]{2,1,0:T(8,128)(2,1)} %bitcast.10, ...), custom_call_target="tpu_custom_call" | custom-call | tf_op jit(solution)/shard_map/block_backward/pallas_call | solution.py:473
  92.9 0.7 copy.10
